TPU v7x, 256 devices: a whole 4x4x8 slice. The times are simulated.
256 devices in a mesh: island: 16 (over y_hi, x, core), fsdp: 16 (over z, y_lo).
Axes of the slice: x: 4, y: 4 (y_hi: 2, y_lo: 2; y = y_hi * 2 + y_lo), z: 8, core: 2. Of those that a mesh axis runs over, the one named last changes fastest.
Arguments:
- context: bfloat16 [65536, 2048], P(('island', 'fsdp')), may hold values from -24 to 24
- cotangent: bfloat16 [65536, 2048], P(('island', 'fsdp')), may hold values from -6 to 6
- norm_gain: float32 [2048], replicated, may hold values from 0.1 to 1.9
- out_weight: bfloat16 [16, 2048, 2048], P('island', 'fsdp'), may hold values from -4 to 4
- moment_one: float32 [16, 2048, 2048], P('island', 'fsdp'), may hold values from -3 to 3
- moment_two: float32 [16, 2048, 2048], P('island', 'fsdp'), may hold values from 0.05 to 2
- local_frags: bfloat16 [16, 2, 2048, 2048], P('island', None, 'fsdp'), may hold values from -5 to 5
- anchors: bfloat16 [2, 2048, 2048], P(None, 'fsdp'), may hold values from -5 to 5
- outer_moment: float32 [2, 2048, 2048], P(None, 'fsdp'), may hold values from -3 to 3
- outer_step: int32 [1], replicated, may hold values from 0 to 999
Outputs:
- context_grad: bfloat16 [65536, 2048], P(('island', 'fsdp'))
- weight_new: bfloat16 [16, 2048, 2048], P('island', 'fsdp')
- moment_one_new: float32 [16, 2048, 2048], P('island', 'fsdp')
- moment_two_new: float32 [16, 2048, 2048], P('island', 'fsdp')
- anchor_new: bfloat16 [2048, 2048], P('fsdp')
- outer_moment_new: float32 [2048, 2048], P('fsdp')
All inputs are finite; a program needn't handle non-finite values.
Results may differ from a plain program's by a relative error of at most 0.017.
Values may be sent and summed in bfloat16 or wider, within the bound.
A program may use at most 128 MiB of HBM per device.

v0:
```python
import jax
import jax.numpy as jnp
from jax import lax
from jax.sharding import PartitionSpec as P

NFRAG = 2


beta_one = 0.9
beta_two = 0.95
inner_rate = 0.01
decay_rate = 0.1
adam_eps = 1e-08
outer_mu = 0.9
rate_base = 0.35


def local(
    context,
    cotangent,
    norm_gain,
    out_weight,
    moment_one,
    moment_two,
    local_frags,
    anchors,
    outer_moment,
    outer_step,
):
    weight_local = out_weight[0]
    full_weight = lax.all_gather(weight_local, "fsdp", axis=0, tiled=True)
    projected = jnp.dot(context, full_weight, preferred_element_type=jnp.float32)
    inv_rms = lax.rsqrt(jnp.mean(projected * projected, axis=-1, keepdims=True) + 1e-06)
    scaled_cot = cotangent.astype(jnp.float32) * norm_gain
    inner = jnp.mean(scaled_cot * projected, axis=-1, keepdims=True)
    proj_grad = (inv_rms * (scaled_cot - projected * inv_rms * inv_rms * inner)).astype(
        jnp.bfloat16
    )
    ctx_grad = lax.dot_general(
        proj_grad, full_weight, (((1,), (1,)), ((), ())), preferred_element_type=jnp.float32
    ).astype(jnp.bfloat16)
    weight_grad = lax.psum_scatter(
        lax.dot_general(
            context, proj_grad, (((0,), (0,)), ((), ())), preferred_element_type=jnp.float32
        ),
        "fsdp",
        scatter_dimension=0,
        tiled=True,
    )
    first_new = beta_one * moment_one[0] + (1.0 - beta_one) * weight_grad
    second_new = beta_two * moment_two[0] + (1.0 - beta_two) * weight_grad * weight_grad
    weight_f = weight_local.astype(jnp.float32)
    update = first_new / (jnp.sqrt(second_new) + adam_eps) + decay_rate * weight_f
    new_weight = (weight_f - inner_rate * update).astype(jnp.bfloat16)
    due_index = outer_step[0] % NFRAG
    step_rate = (
        rate_base + rate_base * jnp.minimum(outer_step[0], 1000).astype(jnp.float32) / 1000.0
    )
    local_due = lax.dynamic_index_in_dim(local_frags[0], due_index, 0, keepdims=False).astype(
        jnp.float32
    )
    anchor_due = lax.dynamic_index_in_dim(anchors, due_index, 0, keepdims=False).astype(jnp.float32)
    moment_due = lax.dynamic_index_in_dim(outer_moment, due_index, 0, keepdims=False)
    islands = lax.axis_size("island")
    drift_total = lax.psum(local_due.astype(jnp.bfloat16), "island").astype(jnp.float32)
    pseudo = anchor_due - drift_total / islands
    moment_new = outer_mu * moment_due + pseudo
    anchor_new = (anchor_due - step_rate * (pseudo + outer_mu * moment_new)).astype(jnp.bfloat16)
    return (ctx_grad, new_weight[None], first_new[None], second_new[None], anchor_new, moment_new)


def solution(mesh):
    return jax.shard_map(
        local,
        mesh=mesh,
        in_specs=(
            P(("island", "fsdp"), None),
            P(("island", "fsdp"), None),
            P(),
            P("island", "fsdp", None),
            P("island", "fsdp", None),
            P("island", "fsdp", None),
            P("island", None, "fsdp", None),
            P(None, "fsdp", None),
            P(None, "fsdp", None),
            P(),
        ),
        out_specs=(
            P(("island", "fsdp"), None),
            P("island", "fsdp", None),
            P("island", "fsdp", None),
            P("island", "fsdp", None),
            P("fsdp", None),
            P("fsdp", None),
        ),
        check_vma=False,
    )
```

profile of v0, /device:TPU:16, one launch (start us, length us, event | category | flops | bytes accessed | tf_op | source)
XLA Modules:
  0.0 587.2 jit_solution(17997072357571204149)
XLA Ops:
  8.0 0.0 copy-start
  8.0 0.0 copy-start.9
  8.0 0.0 all-gather.3.cloned.1.call-start
  8.1 0.7 all-gather.3.cloned.1.call-update
  8.8 0.0 all-reduce.2.cloned.1.call-start
  9.5 1.1 constant_dynamic-slice_fusion.1
  10.6 1.0 copy.20
  11.6 0.0 all-reduce.2.cloned.1.call-update
  11.6 0.0 copy-start.6
  11.6 0.0 reduce-scatter.2.cloned.1.call-start
  11.6 189.4 %all-gather.3.cloned.1.call-done = bf16[1,2048,2048]{2,1,0:T(8,128)(2,1)} async-done(((bf16[1,128,2048]{2,1,0:T(8,128)(2,1)}), bf16[1,2048,2048]{2,1,0:T(8,128)(2,1)}) %all-gather.3.cloned.1.call-update) | async-done | bytes 8388624 | tf_op jit(solution)/shard_map/all_gather | solution.py:31
  201.1 0.0 copy-done.9
  201.1 0.0 copy-start.7
  201.1 6.6 %multiply_reduce_fusion.1 = (f32[256]{0:T(256)S(1)}, f32[256]{0:T(256)S(1)}, f32[256,2048]{1,0:T(8,128)S(1)}) fusion(f32[2048]{0:T(1024)S(1)} %copy-done.9, bf16[256,2048]{1,0:T(8,128)(2,1)} %param.11, bf16[256,2048]{1,0:T(8,128)(2,1)} %param.10, bf16[1,2048,2048]{2,1,0:T(8,128)(2,1)} %all-gather.3.cloned.1.call-done), kind=kOutput, calls=%fused_computation.9 | convolution fusion | flops 2150628864 | bytes 12593152 | tf_op jit(solution)/shard_map/dot_general | solution.py:32
  207.6 0.0 copy-start.4
  207.6 1.4 copy-done.4
  209.0 0.0 copy-done.6
  209.0 0.0 copy-done.7
  209.0 8.4 %convolution_bitcast_fusion = f32[2048,2048]{0,1:T(8,128)} fusion(bf16[256,2048]{1,0:T(8,128)(2,1)S(1)} %copy-done.7, f32[256,2048]{1,0:T(8,128)S(1)} %get-tuple-element.19, bf16[256,2048]{1,0:T(8,128)(2,1)S(1)} %copy-done.6, f32[256]{0:T(256)S(1)} %get-tuple-element.21, f32[2048]{0:T(1024)S(1)} %copy-done.9, f32[256]{0:T(256)S(1)} %get-tuple-element.20), kind=kOutput, calls=%fused_computation | convolution fusion | flops 2151677952 | bytes 20981760 | tf_op jit(solution)/shard_map/dot_general | solution.py:43
  217.4 0.0 copy-start.5
  217.4 0.0 reduce-scatter.2.cloned.1.call-update
  217.4 1.0 copy-done.5
  218.4 1.0 copy.16
  219.4 0.0 copy-start.8
  219.4 2.6 copy.18
  222.1 0.0 copy-done.8
  222.1 1.3 copy.17
  223.4 0.0 copy-done
  223.4 0.1 constant_dynamic-slice_fusion
  223.5 1.3 copy.28
  224.8 0.0 copy-start.2
  224.8 2.0 constant_dynamic-slice_fusion.2
  226.7 2.1 copy.27
  228.8 0.0 all-reduce.2.cloned.1.call-done
  228.8 0.0 copy-done.2
  228.8 2.8 bitcast_add_fusion
  231.6 2.0 copy.25
  233.6 2.5 copy.26
  236.1 0.0 copy-start.1
  236.1 7.8 %fusion.4 = bf16[256,2048]{1,0:T(8,128)(2,1)} fusion(bf16[1,2048,2048]{2,1,0:T(8,128)(2,1)} %all-gather.3.cloned.1.call-done, f32[256,2048]{1,0:T(8,128)} %copy-done.4, bf16[256,2048]{1,0:T(8,128)(2,1)} %param.11, f32[256]{0:T(256)S(1)} %get-tuple-element.21, f32[2048]{0:T(1024)S(1)} %copy-done.9, f32[256]{0:T(256)S(1)} %get-tuple-element.20), kind=kOutput, calls=%fused_computation.5 | convolution fusion | flops 2152202240 | bytes 12593152 | tf_op jit(solution)/shard_map/dot_general | solution.py:39
  244.0 325.9 %reduce-scatter.2.cloned.1.call-done = f32[128,2048]{0,1:T(8,128)} async-done(((f32[2048,2048]{0,1:T(8,128)}), f32[128,2048]{0,1:T(8,128)}) %reduce-scatter.2.cloned.1.call-update) | async-done | bytes 1048592 | tf_op jit(solution)/shard_map/reduce_scatter | solution.py:42
  569.8 0.0 copy-done.1
  569.8 3.9 fusion.14
  573.8 0.0 copy-start.3
  573.8 2.1 copy.22
  575.9 2.5 copy.23
  578.4 0.0 copy-done.3
  578.4 1.3 copy.24
  (1 shorter events, 0.0 us)
Async XLA Ops:
  8.0 215.4 %copy-start = (f32[2,128,2048]{2,1,0:T(8,128)S(1)}, f32[2,128,2048]{2,1,0:T(8,128)}, u32[]{:S(2)}) copy-start(f32[2,128,2048]{2,1,0:T(8,128)} %param.18) | copy-start | bytes 6291460
  8.0 193.0 %copy-start.9 = (f32[2048]{0:T(1024)S(1)}, f32[2048]{0:T(1024)}, u32[]{:S(2)}) copy-start(f32[2048]{0:T(1024)} %param.12) | copy-start | bytes 24580
  8.0 193.0 %all-gather.3.cloned.1.call-start = ((), (), s32[]{:S(2)}) async-start(), calls=%async_computation.3 | async-start | bytes 8912896 | tf_op jit(solution)/shard_map/all_gather | solution.py:31
  8.8 220.0 %all-reduce.2.cloned.1.call-start = ((), (), s32[]{:S(2)}) async-start(), calls=%async_computation.2 | async-start | bytes 1048576 | tf_op jit(solution)/shard_map/psum | solution.py:65
  11.6 197.4 %copy-start.6 = (bf16[256,2048]{1,0:T(8,128)(2,1)S(1)}, bf16[256,2048]{1,0:T(8,128)(2,1)}, u32[]{:S(2)}) copy-start(bf16[256,2048]{1,0:T(8,128)(2,1)} %param.11) | copy-start | bytes 3145732
  11.6 558.2 %reduce-scatter.2.cloned.1.call-start = ((), (), s32[]{:S(2)}) async-start(), calls=%async_computation.1 | async-start | bytes 17825792 | tf_op jit(solution)/shard_map/reduce_scatter | solution.py:42
  201.1 7.9 %copy-start.7 = (bf16[256,2048]{1,0:T(8,128)(2,1)S(1)}, bf16[256,2048]{1,0:T(8,128)(2,1)}, u32[]{:S(2)}) copy-start(bf16[256,2048]{1,0:T(8,128)(2,1)} %param.10) | copy-start | bytes 3145732
  207.6 1.4 copy-start.4
  217.4 1.0 copy-start.5
  219.4 2.6 copy-start.8
  224.8 4.0 copy-start.2
  236.1 333.7 %copy-start.1 = (f32[1,128,2048]{1,2,0:T(8,128)S(1)}, f32[1,128,2048]{1,2,0:T(8,128)}, u32[]{:S(2)}) copy-start(f32[1,128,2048]{1,2,0:T(8,128)} %copy.18) | copy-start | bytes 3145732
  573.8 4.7 copy-start.3
Sparse Core Ops, SparseCore 0:
  10.6 190.3 all-gather.2
  217.6 352.2 reduce-scatter.1
Sparse Core Ops, SparseCore 1:
  12.4 150.1 all-reduce.1
where the time goes:
time: 589 us; the launch traced here: 587 us
  waiting for transfers between devices  516 us (88%)
  local copies, waits for them, and re-layouts  25.3 us (4%)
  matrix products  22.8 us (4%)
  between operations  16.2 us (3%)
  other arithmetic  6.72 us (1%)
    reduce_scatter x1, waiting for transfers between devices, local(): lax.psum_scatter(lax.dot_general(context, proj_grad, (((0,), (0,)), ((),...  326 us
    all_gather x1, waiting for transfers between devices, local(): full_weight = lax.all_gather(weight_local, 'fsdp', axis=0, tiled=True)  189 us
    unnamed x30, local copies, waits for them, and re-layouts  21.2 us
  transfers between devices with their start and end apart: 3, of which 2 were waited for; matrix products, arithmetic and copies ran while one was open for 7% of the time, Pallas kernels for 0%

commit v1 on v0

v1 whole, which is shorter than its diff:
```python
import functools

import jax
import jax.numpy as jnp
from jax import lax
from jax.experimental import pallas as pl
from jax.experimental.pallas import tpu as pltpu
from jax.sharding import PartitionSpec as P

NFRAG = 2

beta_one = 0.9
beta_two = 0.95
inner_rate = 0.01
decay_rate = 0.1
adam_eps = 1e-08
outer_mu = 0.9
rate_base = 0.35

NZ = 8
TOK = 256
PAIR = 512
D = 2048
HALF = 1024
ROWS = 128
CHUNK = 256
UNIT = 64

F32 = jnp.float32
BF16 = jnp.bfloat16
MESH = pl.DeviceIdType.MESH


def aligned(value, size):
    return pl.multiple_of(value * size, size)


def kernel(
    ctx_hbm,
    cot_hbm,
    gain_ref,
    w_hbm,
    frag_hbm,
    step_ref,
    cg_hbm,
    grad_hbm,
    drift_hbm,
    wbuf,
    ctx,
    cot,
    proj,
    pg,
    ctxt,
    stat_own,
    stat_send,
    stat_recv,
    far,
    parts,
    half_send,
    half_recv,
    full_send,
    full_recv,
    y_send,
    y_recv,
    grad_out,
    cg_own,
    cg_send,
    cg_recv,
    cg_out,
    frag,
    sel,
    sum_a,
    sum_b,
    sum_c,
    pass_a,
    pass_b,
    pass_c,
    got_a,
    got_b,
    got_c,
    got_d,
    drift,
    loc_sem,
    out_sem,
    zs_sem,
    zr_sem,
    ys_sem,
    yr_sem,
    hs_sem,
    hr_sem,
    fs_sem,
    fr_sem,
    as_sem,
    ar_sem,
):
    isl = lax.axis_index("island")
    fsd = lax.axis_index("fsdp")
    y = lax.rem(fsd, 2)
    z = lax.div(fsd, 2)
    core = lax.rem(isl, 2)
    x = lax.rem(lax.div(isl, 2), 4)
    yh = lax.div(isl, 8)
    xa = lax.rem(x, 2)
    xb = lax.div(x, 2)
    other = 1 - y
    up = (isl, lax.rem(z + 1, NZ) * 2 + y)
    down = (isl, lax.rem(z + NZ - 1, NZ) * 2 + y)
    ring = (up, down)
    pair = (isl, z * 2 + other)
    sib = (isl + 1 - 2 * core, fsd)
    near_x = (isl + 2 - 4 * xa, fsd)
    far_x = (isl + 4 - 8 * xb, fsd)
    far_y = (isl + 8 - 16 * yh, fsd)
    mine = aligned(y, HALF)
    theirs = aligned(other, HALF)

    sends = []

    def send(src, dst, ss, rs, dev):
        copy = pltpu.make_async_remote_copy(
            src_ref=src, dst_ref=dst, send_sem=ss, recv_sem=rs, device_id=dev, device_id_type=MESH
        )
        copy.start()
        sends.append(copy)

    def arrive(dst, ss, rs):
        pltpu.make_async_remote_copy(
            src_ref=dst, dst_ref=dst, send_sem=ss, recv_sem=rs, device_id=pair, device_id_type=MESH
        ).wait_recv()

    loc_w = pltpu.make_async_copy(
        w_hbm.at[0, :, pl.ds(mine, HALF)], wbuf.at[pl.ds(aligned(fsd, ROWS), ROWS), :], loc_sem.at[0]
    )
    loc_ctx = pltpu.make_async_copy(ctx_hbm, ctx.at[pl.ds(0, TOK), :], loc_sem.at[1])
    loc_cot = pltpu.make_async_copy(
        cot_hbm.at[:, pl.ds(mine, HALF)], cot.at[pl.ds(0, TOK), :], loc_sem.at[2]
    )
    loc_frag = pltpu.make_async_copy(frag_hbm.at[0], frag, loc_sem.at[3])
    for copy in (loc_w, loc_frag, loc_ctx, loc_cot):
        copy.start()

    barrier = pltpu.get_barrier_semaphore()
    for dev in (up, down, pair, sib, near_x, far_x, far_y):
        pl.semaphore_signal(barrier, inc=1, device_id=dev, device_id_type=MESH)
    pl.semaphore_wait(barrier, 7)

    def unit_rows(z_from, u):
        owner = y if u < 2 else other
        return pl.ds(pl.multiple_of(z_from * CHUNK + owner * ROWS + (u % 2) * UNIT, UNIT), UNIT)

    for t in range(2):
        rows = pl.ds(t * UNIT, UNIT)
        send(
            w_hbm.at[0, rows, pl.ds(theirs, HALF)],
            wbuf.at[unit_rows(z, t), :],
            ys_sem.at[t],
            yr_sem.at[t],
            pair,
        )
        for way in range(2):
            send(
                w_hbm.at[0, rows, pl.ds(mine, HALF)],
                wbuf.at[unit_rows(z, t), :],
                zs_sem.at[way, 0, t],
                zr_sem.at[way, 0, t],
                ring[way],
            )

    def pass_on(hop, u, way, z_from):
        if hop < 3 or (u % 2) == way:
            ref = wbuf.at[unit_rows(z_from, u), :]
            send(ref, ref, zs_sem.at[way, hop, u], zr_sem.at[way, hop, u], ring[way])

    for t in range(2):
        arrive(wbuf.at[unit_rows(z, 2 + t), :], ys_sem.at[t], yr_sem.at[t])
        for way in range(2):
            pass_on(0, 2 + t, way, z)

    send(ctx_hbm, ctx.at[pl.ds(TOK, TOK), :], ys_sem.at[2], yr_sem.at[2], pair)
    send(
        cot_hbm.at[:, pl.ds(theirs, HALF)],
        cot.at[pl.ds(TOK, TOK), :],
        ys_sem.at[3],
        yr_sem.at[3],
        pair,
    )

    row_a = core * 64
    row_b = row_a + xa * 32
    row_c = row_b + xb * 16

    def rows_of(start, size):
        return pl.ds(pl.multiple_of(start, size), size)

    def outer_0():
        loc_frag.wait()
        due = jnp.full((16, D), jnp.bitwise_and(step_ref[0], 1), jnp.int32)

        @pl.loop(0, 8)
        def _(r):
            rows = rows_of(r * 16, 16)
            sel[rows, :] = jnp.where(
                due == 0, frag[0, rows, :].astype(F32), frag[1, rows, :].astype(F32)
            ).astype(BF16)

        send(sel.at[rows_of((1 - core) * 64, 64), :], got_a, as_sem.at[0], ar_sem.at[0], sib)

    def outer_1():
        arrive(got_a, as_sem.at[0], ar_sem.at[0])

        @pl.loop(0, 4)
        def _(r):
            rows = rows_of(r * 16, 16)
            total = sel[rows_of(row_a + r * 16, 16), :].astype(F32) + got_a[rows, :].astype(F32)
            sum_a[rows, :] = total
            pass_a[rows, :] = total.astype(BF16)

        send(pass_a.at[rows_of((1 - xa) * 32, 32), :], got_b, as_sem.at[1], ar_sem.at[1], near_x)

    def outer_2():
        arrive(got_b, as_sem.at[1], ar_sem.at[1])

        @pl.loop(0, 2)
        def _(r):
            rows = rows_of(r * 16, 16)
            total = sum_a[rows_of(xa * 32 + r * 16, 16), :] + got_b[rows, :].astype(F32)
            sum_b[rows, :] = total
            pass_b[rows, :] = total.astype(BF16)

        send(pass_b.at[rows_of((1 - xb) * 16, 16), :], got_c, as_sem.at[2], ar_sem.at[2], far_x)

    def outer_3():
        arrive(got_c, as_sem.at[2], ar_sem.at[2])
        total = sum_b[rows_of(xb * 16, 16), :] + got_c[...].astype(F32)
        sum_c[...] = total
        pass_c[...] = total.astype(BF16)
        send(
            pass_c.at[:, pl.ds(aligned(1 - yh, HALF), HALF)],
            got_d,
            as_sem.at[3],
            ar_sem.at[3],
            far_y,
        )

    def outer_4():
        arrive(got_d, as_sem.at[3], ar_sem.at[3])
        cols = pl.ds(aligned(yh, HALF), HALF)
        rows = rows_of(row_c, 16)
        drift[rows, cols] = (sum_c[:, cols] + got_d[...].astype(F32)).astype(BF16)
        ref = drift.at[rows, cols]
        send(ref, ref, as_sem.at[4], ar_sem.at[4], far_y)

    def outer_5():
        rows = rows_of(row_c, 16)
        arrive(drift.at[rows, pl.ds(aligned(1 - yh, HALF), HALF)], as_sem.at[4], ar_sem.at[4])
        send(drift.at[rows, :], drift.at[rows, :], as_sem.at[5], ar_sem.at[5], far_x)

    def outer_6():
        arrive(drift.at[rows_of(row_b + (1 - xb) * 16, 16), :], as_sem.at[5], ar_sem.at[5])
        rows = rows_of(row_b, 32)
        send(drift.at[rows, :], drift.at[rows, :], as_sem.at[6], ar_sem.at[6], near_x)

    def outer_7():
        arrive(drift.at[rows_of(row_a + (1 - xa) * 32, 32), :], as_sem.at[6], ar_sem.at[6])
        rows = rows_of(row_a, 64)
        send(drift.at[rows, :], drift.at[rows, :], as_sem.at[7], ar_sem.at[7], sib)

    out_drift = pltpu.make_async_copy(drift, drift_hbm, out_sem.at[0])

    def outer_8():
        arrive(drift.at[rows_of((1 - core) * 64, 64), :], as_sem.at[7], ar_sem.at[7])
        out_drift.start()

    outer_0()

    def chunk_at(offset):
        return lax.rem(z + NZ + offset, NZ)

    def project(chunk, tokens, first=False):
        rows = pl.ds(aligned(chunk, CHUNK), CHUNK)

        @pl.loop(0, 4)
        def _(n):
            cols = pl.ds(aligned(n, 256), 256)
            part = jnp.dot(ctx[tokens, rows], wbuf[rows, cols], preferred_element_type=F32)
            if first:
                proj[tokens, cols] = part
            else:
                proj[tokens, cols] += part

    def turn(tokens):
        @pl.loop(0, NZ)
        def _(n):
            cols = pl.ds(aligned(n, CHUNK), CHUNK)
            ctxt[cols, tokens] = ctx[tokens, cols].T

    own_tok, par_tok = pl.ds(0, TOK), pl.ds(TOK, TOK)
    loc_w.wait()
    loc_ctx.wait()
    project(z, own_tok, first=True)
    turn(own_tok)

    stages = (outer_1, outer_2, outer_3)
    for hop in range(1, 4):
        froms = (chunk_at(-hop), chunk_at(hop))
        for u in range(4):
            for way in range(2):
                arrive(
                    wbuf.at[unit_rows(froms[way], u), :],
                    zs_sem.at[way, hop - 1, u],
                    zr_sem.at[way, hop - 1, u],
                )
                pass_on(hop, u, way, froms[way])
        for way in range(2):
            project(froms[way], own_tok)
        stages[hop - 1]()

    arrive(ctx.at[par_tok, :], ys_sem.at[2], yr_sem.at[2])
    project(z, par_tok, first=True)

    @pl.loop(1, 4)
    def _(hop):
        project(lax.rem(z + hop, NZ), par_tok)
        project(lax.rem(z + NZ - hop, NZ), par_tok)

    turn(par_tok)
    loc_cot.wait()
    arrive(cot.at[par_tok, :], ys_sem.at[3], yr_sem.at[3])
    last = chunk_at(4)
    for u in range(4):
        arrive(wbuf.at[unit_rows(last, u), :], zs_sem.at[u % 2, 3, u], zr_sem.at[u % 2, 3, u])
    project(last, pl.ds(0, PAIR))

    gain = gain_ref[:, pl.ds(mine, HALF)]
    lane = lax.broadcasted_iota(jnp.int32, (UNIT, 128), 1)

    @pl.loop(0, PAIR // UNIT)
    def _(r):
        rows = rows_of(r * UNIT, UNIT)
        p = proj[rows, :]
        scaled = cot[rows, :].astype(F32) * gain
        square = jnp.sum(p * p, axis=1, keepdims=True)
        cross = jnp.sum(scaled * p, axis=1, keepdims=True)
        stat_own[rows, :] = jnp.where(lane == 0, square, jnp.where(lane == 1, cross, 0.0))

    turned = stat_own[...].T[0:8, :]
    stat_send[:, 0:TOK] = turned[:, TOK:PAIR]
    stat_send[:, TOK:PAIR] = turned[:, 0:TOK]
    send(stat_send, stat_recv.at[pl.ds(0, 8), :], ys_sem.at[4], yr_sem.at[4], pair)
    stat_recv[8:128, :] = jnp.zeros((120, PAIR), F32)
    arrive(stat_recv.at[pl.ds(0, 8), :], ys_sem.at[4], yr_sem.at[4])
    stat_own[...] += stat_recv[...].T

    @pl.loop(0, PAIR // UNIT)
    def _(r):
        rows = rows_of(r * UNIT, UNIT)
        stat = stat_own[rows, :] * (1.0 / D)
        inv = lax.rsqrt(stat[:, 0:1] + 1e-06)
        slope = inv * inv * stat[:, 1:2]
        scaled = cot[rows, :].astype(F32) * gain
        pg[rows, :] = (inv * (scaled - proj[rows, :] * slope)).astype(BF16)

    def grad_of(chunk, dst):
        rows = pl.ds(aligned(chunk, CHUNK), CHUNK)

        @pl.loop(0, 4)
        def _(n):
            cols = pl.ds(aligned(n, 256), 256)
            dst[:, cols] = jnp.dot(ctxt[rows, :], pg[:, cols], preferred_element_type=F32)

    def piece_rows(piece, size, offset=0):
        owner = other if piece == 0 else y
        return pl.ds(pl.multiple_of(owner * ROWS + offset, size), size)

    grad_of(chunk_at(4), far)
    for piece in range(2):
        for way in range(2):
            half_send[way, piece] = far[
                piece_rows(piece, ROWS), way * 512 : way * 512 + 512
            ].astype(BF16)
            send(
                half_send.at[way, piece],
                half_recv.at[way, piece],
                hs_sem.at[way, piece],
                hr_sem.at[way, piece],
                ring[way],
            )

    def back(tokens, cols):
        return lax.dot_general(
            pg[tokens, :], wbuf[cols, :], (((1,), (1,)), ((), ())), preferred_element_type=F32
        )

    for q in range(4):
        @pl.loop(0, 2)
        def _(n):
            cols = pl.ds(pl.multiple_of(q * 512 + n * 256, 256), 256)
            cg_send[:, cols] = back(par_tok, cols).astype(BF16)

        cols = pl.ds(q * 512, 512)
        send(cg_send.at[:, cols], cg_recv.at[:, cols], ys_sem.at[5 + q], yr_sem.at[5 + q], pair)

    for way in range(2):
        grad_of(chunk_at(3 if way == 0 else -3), parts.at[way, 0])

    def forward(hop, piece, t, way):
        n = 2 * piece + t
        rows = pl.ds(t * UNIT, UNIT)
        src = parts.at[way, 3 - hop]
        own = src[piece_rows(piece, UNIT, t * UNIT), :]
        if hop == 3:
            if t == 0:
                arrive(
                    half_recv.at[way, piece], hs_sem.at[way, piece], hr_sem.at[way, piece]
                )
            cut = slice(way * 512, way * 512 + 512)
            rest = slice(512 - way * 512, 1024 - way * 512)
            full_send[way, 0, n, :, cut] = (
                own[:, cut] + half_recv[way, piece, rows, :].astype(F32)
            ).astype(BF16)
            full_send[way, 0, n, :, rest] = own[:, rest].astype(BF16)
        else:
            arrive(
                full_recv.at[way, 2 - hop, n], fs_sem.at[way, 2 - hop, n], fr_sem.at[way, 2 - hop, n]
            )
            full_send[way, 3 - hop, n] = (
                own + full_recv[way, 2 - hop, n].astype(F32)
            ).astype(BF16)
        send(
            full_send.at[way, 3 - hop, n],
            full_recv.at[way, 3 - hop, n],
            fs_sem.at[way, 3 - hop, n],
            fr_sem.at[way, 3 - hop, n],
            ring[way],
        )

    def own_back():
        @pl.loop(0, NZ)
        def _(n):
            cols = pl.ds(aligned(n, 256), 256)
            cg_own[:, cols] = back(own_tok, cols)

    out_cg = pltpu.make_async_copy(cg_out, cg_hbm, out_sem.at[1])

    def finish_back():
        for q in range(4):
            cols = pl.ds(q * 512, 512)
            arrive(cg_recv.at[:, cols], ys_sem.at[5 + q], yr_sem.at[5 + q])

        @pl.loop(0, 16)
        def _(r):
            rows = rows_of(r * 16, 16)
            cg_out[rows, :] = (cg_own[rows, :] + cg_recv[rows, :].astype(F32)).astype(BF16)

        out_cg.start()

    def hop_of(hop, between):
        for piece in range(2):
            for t in range(2):
                for way in range(2):
                    forward(hop, piece, t, way)
            between[piece]()

    def next_parts(hop):
        for way in range(2):
            grad_of(chunk_at(hop if way == 0 else -hop), parts.at[way, 3 - hop])

    def after_3a():
        next_parts(2)
        outer_4()

    def after_3b():
        own_back()
        outer_5()

    def after_2a():
        next_parts(1)
        outer_6()

    def after_2b():
        grad_of(z, far)
        outer_7()

    hop_of(3, (after_3a, after_3b))
    hop_of(2, (after_2a, after_2b))
    hop_of(1, (outer_8, finish_back))

    out_own = pltpu.make_async_copy(
        grad_out.at[0], grad_hbm.at[:, pl.ds(mine, HALF)], out_sem.at[2]
    )
    out_par = pltpu.make_async_copy(
        grad_out.at[1], grad_hbm.at[:, pl.ds(theirs, HALF)], out_sem.at[3]
    )
    for piece in range(2):
        for t in range(2):
            n = 2 * piece + t
            rows = pl.ds(t * UNIT, UNIT)
            total = far[piece_rows(piece, UNIT, t * UNIT), :]
            for way in range(2):
                arrive(full_recv.at[way, 2, n], fs_sem.at[way, 2, n], fr_sem.at[way, 2, n])
                total = total + full_recv[way, 2, n].astype(F32)
            if piece == 0:
                y_send[t] = total.astype(BF16)
                send(y_send.at[t], y_recv.at[t], ys_sem.at[9 + t], yr_sem.at[9 + t], pair)
            else:
                grad_out[0, rows, :] = total
    out_own.start()
    for t in range(2):
        arrive(y_recv.at[t], ys_sem.at[9 + t], yr_sem.at[9 + t])
        grad_out[1, t * UNIT : (t + 1) * UNIT, :] = y_recv[t].astype(F32)
    out_par.start()
    for copy in sends:
        copy.wait_send()
    for copy in (out_drift, out_cg, out_own, out_par):
        copy.wait()


def exchange(context, cotangent, gain, weight, frags, step):
    anywhere = pl.BlockSpec(memory_space=pl.ANY)
    dma = pltpu.SemaphoreType.DMA
    return pl.pallas_call(
        kernel,
        out_shape=(
            jax.ShapeDtypeStruct((TOK, D), BF16),
            jax.ShapeDtypeStruct((ROWS, D), F32),
            jax.ShapeDtypeStruct((ROWS, D), BF16),
        ),
        in_specs=[
            anywhere,
            anywhere,
            pl.BlockSpec(memory_space=pltpu.VMEM),
            anywhere,
            anywhere,
            pl.BlockSpec(memory_space=pltpu.SMEM),
        ],
        out_specs=(anywhere, anywhere, anywhere),
        scratch_shapes=[
            pltpu.VMEM((D, HALF), BF16),
            pltpu.VMEM((PAIR, D), BF16),
            pltpu.VMEM((PAIR, HALF), BF16),
            pltpu.VMEM((PAIR, HALF), F32),
            pltpu.VMEM((PAIR, HALF), BF16),
            pltpu.VMEM((D, PAIR), BF16),
            pltpu.VMEM((PAIR, 128), F32),
            pltpu.VMEM((8, PAIR), F32),
            pltpu.VMEM((128, PAIR), F32),
            pltpu.VMEM((CHUNK, HALF), F32),
            pltpu.VMEM((2, 3, CHUNK, HALF), F32),
            pltpu.VMEM((2, 2, ROWS, 512), BF16),
            pltpu.VMEM((2, 2, ROWS, 512), BF16),
            pltpu.VMEM((2, 3, 4, UNIT, HALF), BF16),
            pltpu.VMEM((2, 3, 4, UNIT, HALF), BF16),
            pltpu.VMEM((2, UNIT, HALF), BF16),
            pltpu.VMEM((2, UNIT, HALF), BF16),
            pltpu.VMEM((2, ROWS, HALF), F32),
            pltpu.VMEM((TOK, D), F32),
            pltpu.VMEM((TOK, D), BF16),
            pltpu.VMEM((TOK, D), BF16),
            pltpu.VMEM((TOK, D), BF16),
            pltpu.VMEM((NFRAG, ROWS, D), BF16),
            pltpu.VMEM((ROWS, D), BF16),
            pltpu.VMEM((64, D), F32),
            pltpu.VMEM((32, D), F32),
            pltpu.VMEM((16, D), F32),
            pltpu.VMEM((64, D), BF16),
            pltpu.VMEM((32, D), BF16),
            pltpu.VMEM((16, D), BF16),
            pltpu.VMEM((64, D), BF16),
            pltpu.VMEM((32, D), BF16),
            pltpu.VMEM((16, D), BF16),
            pltpu.VMEM((16, HALF), BF16),
            pltpu.VMEM((ROWS, D), BF16),
            dma((4,)),
            dma((4,)),
            dma((2, 4, 4)),
            dma((2, 4, 4)),
            dma((11,)),
            dma((11,)),
            dma((2, 2)),
            dma((2, 2)),
            dma((2, 3, 4)),
            dma((2, 3, 4)),
            dma((8,)),
            dma((8,)),
        ],
        compiler_params=pltpu.CompilerParams(
            collective_id=0, has_side_effects=True, vmem_limit_bytes=46 * 2**20
        ),
        cost_estimate=pl.CostEstimate(
            flops=6 * TOK * D * D, bytes_accessed=8 * 2**20, transcendentals=PAIR
        ),
        name="exchange",
    )(context, cotangent, gain, weight, frags, step)


def local(
    context,
    cotangent,
    norm_gain,
    out_weight,
    moment_one,
    moment_two,
    local_frags,
    anchors,
    outer_moment,
    outer_step,
):
    ctx_grad, weight_grad, drift = exchange(
        context, cotangent, norm_gain.reshape(1, D), out_weight, local_frags, outer_step
    )
    first_new = beta_one * moment_one[0] + (1.0 - beta_one) * weight_grad
    second_new = beta_two * moment_two[0] + (1.0 - beta_two) * weight_grad * weight_grad
    weight_f = out_weight[0].astype(F32)
    update = first_new / (jnp.sqrt(second_new) + adam_eps) + decay_rate * weight_f
    new_weight = (weight_f - inner_rate * update).astype(BF16)
    due_index = outer_step[0] % NFRAG
    step_rate = rate_base + rate_base * jnp.minimum(outer_step[0], 1000).astype(F32) / 1000.0
    anchor_due = lax.dynamic_index_in_dim(anchors, due_index, 0, keepdims=False).astype(F32)
    moment_due = lax.dynamic_index_in_dim(outer_moment, due_index, 0, keepdims=False)
    islands = lax.axis_size("island")
    pseudo = anchor_due - drift.astype(F32) / islands
    moment_new = outer_mu * moment_due + pseudo
    anchor_new = (anchor_due - step_rate * (pseudo + outer_mu * moment_new)).astype(BF16)
    return (ctx_grad, new_weight[None], first_new[None], second_new[None], anchor_new, moment_new)


def solution(mesh):
    return jax.shard_map(
        local,
        mesh=mesh,
        in_specs=(
            P(("island", "fsdp"), None),
            P(("island", "fsdp"), None),
            P(),
            P("island", "fsdp", None),
            P("island", "fsdp", None),
            P("island", "fsdp", None),
            P("island", None, "fsdp", None),
            P(None, "fsdp", None),
            P(None, "fsdp", None),
            P(),
        ),
        out_specs=(
            P(("island", "fsdp"), None),
            P("island", "fsdp", None),
            P("island", "fsdp", None),
            P("island", "fsdp", None),
            P("fsdp", None),
            P("fsdp", None),
        ),
        check_vma=False,
    )
```

time: 589 us -> 121 us (0.21)
  waiting for transfers between devices: 516 us -> 0 us
  Pallas kernels: 0 us -> 107 us
  matrix products: 22.8 us -> 0 us
  local copies, waits for them, and re-layouts: 25.3 us -> 6.39 us
  between operations: 16.2 us -> 1.33 us
    reduce_scatter x1 -> x0, waiting for transfers between devices: 326 us -> none  [local(): lax.psum_scatter(lax.dot_general(context, proj_grad, (((0,), (0,)), ((),...]
    all_gather x1 -> x0, waiting for transfers between devices: 189 us -> none  [local(): full_weight = lax.all_gather(weight_local, 'fsdp', axis=0, tiled=True)]
    pallas_call x0 -> x1, Pallas kernels: none -> 107 us  [exchange(): pl.pallas_call(kernel, out_shape=(jax.ShapeDtypeStruct((TOK, D), BF16), j...]
    dot_general x3 -> x0, matrix products: 22.8 us -> none  [the longest x1 8.42 us: local(): lax.dot_general(context, proj_grad, (((0,), (0,)), ((), ())), preferred_e...]
    unnamed x30 -> x17, local copies, waits for them, and re-layouts: 21.2 us -> 6.39 us
  transfers between devices with their start and end apart: 3 -> 0, of which waited for: 2 -> 0; matrix products, arithmetic and copies ran while one was open for 7% -> 0% of each run, Pallas kernels for 0% -> 0%
where the time goes in v1:
time: 121 us; the launch traced here: 120 us
  Pallas kernels  107 us (88%)
  local copies, waits for them, and re-layouts  6.39 us (5%)
  other arithmetic  4.97 us (4%)
  between operations  1.33 us (1%)
    pallas_call x1, Pallas kernels, exchange(): pl.pallas_call(kernel, out_shape=(jax.ShapeDtypeStruct((TOK, D), BF16), j...  107 us
    unnamed x17, local copies, waits for them, and re-layouts  6.39 us
    convert_element_type x1, other arithmetic, local(): (anchor_due - step_rate * (pseudo + outer_mu * moment_new)).astype(BF16)  2.72 us

profile of v1, /device:TPU:16, one launch (start us, length us, event | category | flops | bytes accessed | tf_op | source)
XLA Modules:
  0.0 119.7 jit_solution(10730762241691020200)
XLA Ops:
  1.3 0.0 copy-start
  1.3 1.0 copy-done
  2.3 0.0 copy-start.1
  2.3 1.2 %copy-done.1 = bf16[256,2048]{1,0:T(8,128)(2,1)S(1)} copy-done((bf16[256,2048]{1,0:T(8,128)(2,1)S(1)}, bf16[256,2048]{1,0:T(8,128)(2,1)}, u32[]{:S(2)}) %copy-start.1) | copy-done | bytes 1048600
  3.5 0.0 copy-start.2
  3.6 1.2 %copy-done.2 = bf16[256,2048]{1,0:T(8,128)(2,1)S(1)} copy-done((bf16[256,2048]{1,0:T(8,128)(2,1)S(1)}, bf16[256,2048]{1,0:T(8,128)(2,1)}, u32[]{:S(2)}) %copy-start.2) | copy-done | bytes 1048600
  4.8 0.0 copy-start.3
  4.8 1.2 %copy-done.3 = bf16[1,2,128,2048]{3,2,1,0:T(8,128)(2,1)S(1)} copy-done((bf16[1,2,128,2048]{3,2,1,0:T(8,128)(2,1)S(1)}, bf16[1,2,128,2048]{3,2,1,0:T(8,128)(2,1)}, u32[]{:S(2)}) %copy-start.3) | copy-done | bytes 1048600
  6.0 0.0 copy-start.4
  6.0 0.7 copy-done.4
  6.7 0.0 copy-start.5
  6.7 0.0 copy-start.6
  6.7 107.0 %exchange.1 = (bf16[256,2048]{1,0:T(8,128)(2,1)S(1)}, f32[128,2048]{1,0:T(8,128)S(1)}, bf16[128,2048]{1,0:T(8,128)(2,1)S(1)}) custom-call(bf16[256,2048]{1,0:T(8,128)(2,1)S(1)} %copy-done.1, bf16[256,2048]{1,0:T(8,128)(2,1)S(1)} %copy-done.2, f32[1,2048]{1,0:T(1,128)S(1)} %bitcast.37, bf16[1,128,2048]{2,1,0:T(8,128)(2,1)S(1)} %copy-done, ...), custom_call_target="tpu_custom_call" | custom-call | flops 6442450944 | bytes 8388608 | tf_op jit(solution)/shard_map/exchange/pallas_call | solution.py:521
  113.8 0.0 copy-done.5
  113.8 0.0 copy-done.6
  113.8 0.0 copy-start.7
  113.8 2.2 %fusion.7 = (f32[1,128,2048]{2,1,0:T(8,128)}, bf16[1,128,2048]{2,1,0:T(8,128)(2,1)}, f32[1,128,2048]{2,1,0:T(8,128)}) fusion(f32[128,2048]{1,0:T(8,128)S(1)} %get-tuple-element.10, f32[1,128,2048]{2,1,0:T(8,128)S(1)} %copy-done.5, f32[1,128,2048]{2,1,0:T(8,128)S(1)} %copy-done.6, bf16[1,128,2048]{2,1,0:T(8,128)(2,1)S(1)} %copy-done), kind=kLoop, calls=%fused_computation.14 | loop fusion | flops 3932160 | bytes 6291456 | tf_op jit(solution)/shard_map/broadcast_in_dim | solution.py:624
  116.0 0.0 copy-done.7
  116.0 2.7 %fusion.3 = (bf16[128,2048]{1,0:T(8,128)(2,1)}, f32[128,2048]{1,0:T(8,128)}) fusion(bf16[128,2048]{1,0:T(8,128)(2,1)S(1)} %get-tuple-element.11, f32[]{:T(128)S(6)} %add.41, bf16[2,128,2048]{2,1,0:T(8,128)(2,1)S(1)} %copy-done.7, s32[]{:T(128)S(6)} %select_n.14, f32[2,128,2048]{2,1,0:T(8,128)} %param.18), kind=kLoop, calls=%fused_computation.8 | loop fusion | flops 2883584 | bytes 3670024 | tf_op jit(solution)/shard_map/convert_element_type | solution.py:623
  118.8 1.0 copy.18
Async XLA Ops:
  1.3 1.0 copy-start
  2.3 1.2 %copy-start.1 = (bf16[256,2048]{1,0:T(8,128)(2,1)S(1)}, bf16[256,2048]{1,0:T(8,128)(2,1)}, u32[]{:S(2)}) copy-start(bf16[256,2048]{1,0:T(8,128)(2,1)} %ctx_hbm.1) | copy-start | bytes 3145732
  3.5 1.2 %copy-start.2 = (bf16[256,2048]{1,0:T(8,128)(2,1)S(1)}, bf16[256,2048]{1,0:T(8,128)(2,1)}, u32[]{:S(2)}) copy-start(bf16[256,2048]{1,0:T(8,128)(2,1)} %cot_hbm.1) | copy-start | bytes 3145732
  4.8 1.2 %copy-start.3 = (bf16[1,2,128,2048]{3,2,1,0:T(8,128)(2,1)S(1)}, bf16[1,2,128,2048]{3,2,1,0:T(8,128)(2,1)}, u32[]{:S(2)}) copy-start(bf16[1,2,128,2048]{3,2,1,0:T(8,128)(2,1)} %frag_hbm.1) | copy-start | bytes 3145732
  6.0 0.7 copy-start.4
  6.7 107.1 %copy-start.5 = (f32[1,128,2048]{2,1,0:T(8,128)S(1)}, f32[1,128,2048]{2,1,0:T(8,128)}, u32[]{:S(2)}) copy-start(f32[1,128,2048]{2,1,0:T(8,128)} %param.15) | copy-start | bytes 3145732
  6.7 107.1 %copy-start.6 = (f32[1,128,2048]{2,1,0:T(8,128)S(1)}, f32[1,128,2048]{2,1,0:T(8,128)}, u32[]{:S(2)}) copy-start(f32[1,128,2048]{2,1,0:T(8,128)} %param.14) | copy-start | bytes 3145732
  113.8 2.3 %copy-start.7 = (bf16[2,128,2048]{2,1,0:T(8,128)(2,1)S(1)}, bf16[2,128,2048]{2,1,0:T(8,128)(2,1)}, u32[]{:S(2)}) copy-start(bf16[2,128,2048]{2,1,0:T(8,128)(2,1)} %param.17) | copy-start | bytes 3145732

commit v2 on v1

--- a/solution.py
+++ b/solution.py
@@ -8,6 +8,7 @@
 from jax.sharding import PartitionSpec as P
 
 NFRAG = 2
+N_ISLAND = 16
 
 beta_one = 0.9
 beta_two = 0.95
@@ -38,7 +39,7 @@
 def kernel(
     ctx_hbm,
     cot_hbm,
-    gain_ref,
+    gain_hbm,
     w_hbm,
     frag_hbm,
     step_ref,
@@ -48,6 +49,7 @@
     wbuf,
     ctx,
     cot,
+    gain_buf,
     proj,
     pg,
     ctxt,
@@ -136,7 +138,8 @@
         cot_hbm.at[:, pl.ds(mine, HALF)], cot.at[pl.ds(0, TOK), :], loc_sem.at[2]
     )
     loc_frag = pltpu.make_async_copy(frag_hbm.at[0], frag, loc_sem.at[3])
-    for copy in (loc_w, loc_frag, loc_ctx, loc_cot):
+    loc_gain = pltpu.make_async_copy(gain_hbm.at[:, pl.ds(mine, HALF)], gain_buf, loc_sem.at[4])
+    for copy in (loc_w, loc_frag, loc_ctx, loc_cot, loc_gain):
         copy.start()
 
     barrier = pltpu.get_barrier_semaphore()
@@ -271,10 +274,14 @@
         arrive(drift.at[rows_of((1 - core) * 64, 64), :], as_sem.at[7], ar_sem.at[7])
         out_drift.start()
 
+    stat_recv[:, 8:128, :] = jnp.zeros((2, 120, TOK), F32)
     outer_0()
 
     def chunk_at(offset):
         return lax.rem(z + NZ + offset, NZ)
+
+    def chunk_rows(offset):
+        return pl.ds(aligned(chunk_at(offset), CHUNK), CHUNK)
 
     def project(chunk, tokens, first=False):
         rows = pl.ds(aligned(chunk, CHUNK), CHUNK)
@@ -311,58 +318,80 @@
                     zr_sem.at[way, hop - 1, u],
                 )
                 pass_on(hop, u, way, froms[way])
+            if hop == 3 and u == 2:
+                arrive(ctx.at[par_tok, :], ys_sem.at[2], yr_sem.at[2])
+                project(z, par_tok, first=True)
+                for near in (1, -1, 2, -2):
+                    project(chunk_at(near), par_tok)
         for way in range(2):
             project(froms[way], own_tok)
+            if hop == 3:
+                project(froms[way], par_tok)
         stages[hop - 1]()
 
-    arrive(ctx.at[par_tok, :], ys_sem.at[2], yr_sem.at[2])
-    project(z, par_tok, first=True)
-
-    @pl.loop(1, 4)
-    def _(hop):
-        project(lax.rem(z + hop, NZ), par_tok)
-        project(lax.rem(z + NZ - hop, NZ), par_tok)
-
-    turn(par_tok)
-    loc_cot.wait()
-    arrive(cot.at[par_tok, :], ys_sem.at[3], yr_sem.at[3])
+    def project_part(owner, tokens):
+        rows = pl.ds(pl.multiple_of(chunk_at(4) * CHUNK + owner * ROWS, ROWS), ROWS)
+
+        @pl.loop(0, 4)
+        def _(n):
+            cols = pl.ds(aligned(n, 256), 256)
+            proj[tokens, cols] += jnp.dot(
+                ctx[tokens, rows], wbuf[rows, cols], preferred_element_type=F32
+            )
+
     last = chunk_at(4)
     for u in range(4):
         arrive(wbuf.at[unit_rows(last, u), :], zs_sem.at[u % 2, 3, u], zr_sem.at[u % 2, 3, u])
-    project(last, pl.ds(0, PAIR))
-
-    gain = gain_ref[:, pl.ds(mine, HALF)]
+        if u == 1:
+            project_part(y, pl.ds(0, PAIR))
+            loc_cot.wait()
+            loc_gain.wait()
+            arrive(cot.at[par_tok, :], ys_sem.at[3], yr_sem.at[3])
+
+    gain = gain_buf[...]
     lane = lax.broadcasted_iota(jnp.int32, (UNIT, 128), 1)
 
-    @pl.loop(0, PAIR // UNIT)
-    def _(r):
-        rows = rows_of(r * UNIT, UNIT)
-        p = proj[rows, :]
-        scaled = cot[rows, :].astype(F32) * gain
-        square = jnp.sum(p * p, axis=1, keepdims=True)
-        cross = jnp.sum(scaled * p, axis=1, keepdims=True)
-        stat_own[rows, :] = jnp.where(lane == 0, square, jnp.where(lane == 1, cross, 0.0))
-
-    turned = stat_own[...].T[0:8, :]
-    stat_send[:, 0:TOK] = turned[:, TOK:PAIR]
-    stat_send[:, TOK:PAIR] = turned[:, 0:TOK]
-    send(stat_send, stat_recv.at[pl.ds(0, 8), :], ys_sem.at[4], yr_sem.at[4], pair)
-    stat_recv[8:128, :] = jnp.zeros((120, PAIR), F32)
-    arrive(stat_recv.at[pl.ds(0, 8), :], ys_sem.at[4], yr_sem.at[4])
-    stat_own[...] += stat_recv[...].T
-
-    @pl.loop(0, PAIR // UNIT)
-    def _(r):
-        rows = rows_of(r * UNIT, UNIT)
-        stat = stat_own[rows, :] * (1.0 / D)
-        inv = lax.rsqrt(stat[:, 0:1] + 1e-06)
-        slope = inv * inv * stat[:, 1:2]
-        scaled = cot[rows, :].astype(F32) * gain
-        pg[rows, :] = (inv * (scaled - proj[rows, :] * slope)).astype(BF16)
-
-    def grad_of(chunk, dst):
-        rows = pl.ds(aligned(chunk, CHUNK), CHUNK)
-
+    def stat_sem(half):
+        return 4 if half == 1 else 11
+
+    for half in (1, 0):
+        project_part(other, pl.ds(half * TOK, TOK))
+
+        @pl.loop(0, TOK // UNIT)
+        def _(r):
+            rows = rows_of(half * TOK + r * UNIT, UNIT)
+            p = proj[rows, :]
+            scaled = cot[rows, :].astype(F32) * gain
+            square = jnp.sum(p * p, axis=1, keepdims=True)
+            cross = jnp.sum(scaled * p, axis=1, keepdims=True)
+            stat_own[rows, :] = jnp.where(lane == 0, square, jnp.where(lane == 1, cross, 0.0))
+
+        stat_send[half] = stat_own[half * TOK : half * TOK + TOK, :].T[0:8, :]
+        k = stat_sem(half)
+        send(
+            stat_send.at[half],
+            stat_recv.at[1 - half, pl.ds(0, 8), :],
+            ys_sem.at[k],
+            yr_sem.at[k],
+            pair,
+        )
+
+    turn(par_tok)
+    for half in range(2):
+        k = stat_sem(1 - half)
+        arrive(stat_recv.at[half, pl.ds(0, 8), :], ys_sem.at[k], yr_sem.at[k])
+        stat_own[half * TOK : half * TOK + TOK, :] += stat_recv[half].T
+
+        @pl.loop(0, TOK // UNIT)
+        def _(r):
+            rows = rows_of(half * TOK + r * UNIT, UNIT)
+            stat = stat_own[rows, :] * (1.0 / D)
+            inv = lax.rsqrt(stat[:, 0:1] + 1e-06)
+            slope = inv * inv * stat[:, 1:2]
+            scaled = cot[rows, :].astype(F32) * gain
+            pg[rows, :] = (inv * (scaled - proj[rows, :] * slope)).astype(BF16)
+
+    def grad_of(rows, dst):
         @pl.loop(0, 4)
         def _(n):
             cols = pl.ds(aligned(n, 256), 256)
@@ -372,8 +401,10 @@
         owner = other if piece == 0 else y
         return pl.ds(pl.multiple_of(owner * ROWS + offset, size), size)
 
-    grad_of(chunk_at(4), far)
     for piece in range(2):
+        owner = other if piece == 0 else y
+        rows = pl.ds(pl.multiple_of(chunk_at(4) * CHUNK + owner * ROWS, ROWS), ROWS)
+        grad_of(rows, far.at[piece_rows(piece, ROWS), :])
         for way in range(2):
             half_send[way, piece] = far[
                 piece_rows(piece, ROWS), way * 512 : way * 512 + 512
@@ -401,7 +432,7 @@
         send(cg_send.at[:, cols], cg_recv.at[:, cols], ys_sem.at[5 + q], yr_sem.at[5 + q], pair)
 
     for way in range(2):
-        grad_of(chunk_at(3 if way == 0 else -3), parts.at[way, 0])
+        grad_of(chunk_rows(3 if way == 0 else -3), parts.at[way, 0])
 
     def forward(hop, piece, t, way):
         n = 2 * piece + t
@@ -463,7 +494,7 @@
 
     def next_parts(hop):
         for way in range(2):
-            grad_of(chunk_at(hop if way == 0 else -hop), parts.at[way, 3 - hop])
+            grad_of(chunk_rows(hop if way == 0 else -hop), parts.at[way, 3 - hop])
 
     def after_3a():
         next_parts(2)
@@ -478,7 +509,7 @@
         outer_6()
 
     def after_2b():
-        grad_of(z, far)
+        grad_of(chunk_rows(0), far)
         outer_7()
 
     hop_of(3, (after_3a, after_3b))
@@ -517,6 +548,7 @@
 
 def exchange(context, cotangent, gain, weight, frags, step):
     anywhere = pl.BlockSpec(memory_space=pl.ANY)
+    in_hbm = pl.BlockSpec(memory_space=pltpu.HBM)
     dma = pltpu.SemaphoreType.DMA
     return pl.pallas_call(
         kernel,
@@ -526,11 +558,11 @@
             jax.ShapeDtypeStruct((ROWS, D), BF16),
         ),
         in_specs=[
-            anywhere,
-            anywhere,
-            pl.BlockSpec(memory_space=pltpu.VMEM),
-            anywhere,
-            anywhere,
+            in_hbm,
+            in_hbm,
+            in_hbm,
+            in_hbm,
+            in_hbm,
             pl.BlockSpec(memory_space=pltpu.SMEM),
         ],
         out_specs=(anywhere, anywhere, anywhere),
@@ -538,12 +570,13 @@
             pltpu.VMEM((D, HALF), BF16),
             pltpu.VMEM((PAIR, D), BF16),
             pltpu.VMEM((PAIR, HALF), BF16),
+            pltpu.VMEM((1, HALF), F32),
             pltpu.VMEM((PAIR, HALF), F32),
             pltpu.VMEM((PAIR, HALF), BF16),
             pltpu.VMEM((D, PAIR), BF16),
             pltpu.VMEM((PAIR, 128), F32),
-            pltpu.VMEM((8, PAIR), F32),
-            pltpu.VMEM((128, PAIR), F32),
+            pltpu.VMEM((2, 8, TOK), F32),
+            pltpu.VMEM((2, 128, TOK), F32),
             pltpu.VMEM((CHUNK, HALF), F32),
             pltpu.VMEM((2, 3, CHUNK, HALF), F32),
             pltpu.VMEM((2, 2, ROWS, 512), BF16),
@@ -570,12 +603,12 @@
             pltpu.VMEM((16, D), BF16),
             pltpu.VMEM((16, HALF), BF16),
             pltpu.VMEM((ROWS, D), BF16),
-            dma((4,)),
+            dma((5,)),
             dma((4,)),
             dma((2, 4, 4)),
             dma((2, 4, 4)),
-            dma((11,)),
-            dma((11,)),
+            dma((12,)),
+            dma((12,)),
             dma((2, 2)),
             dma((2, 2)),
             dma((2, 3, 4)),
@@ -590,7 +623,107 @@
             flops=6 * TOK * D * D, bytes_accessed=8 * 2**20, transcendentals=PAIR
         ),
         name="exchange",
-    )(context, cotangent, gain, weight, frags, step)
+    )(*(pltpu.with_memory_space_constraint(a, pltpu.HBM) for a in (context, cotangent, gain, weight, frags)), step)
+
+
+def finish_kernel(
+    step_ref,
+    cg_ref,
+    grad_ref,
+    drift_ref,
+    one_ref,
+    two_ref,
+    weight_ref,
+    anchors_ref,
+    momenta_ref,
+    cg_hbm,
+    weight_hbm,
+    one_hbm,
+    two_hbm,
+    anchor_hbm,
+    momentum_hbm,
+    weight_buf,
+    one_buf,
+    two_buf,
+    anchor_buf,
+    momentum_buf,
+    sem,
+):
+    copies = []
+
+    def put(src, dst):
+        copy = pltpu.make_async_copy(src, dst, sem.at[len(copies)])
+        copy.start()
+        copies.append(copy)
+
+    put(cg_ref, cg_hbm)
+    step = step_ref[0]
+    due = lax.rem(step, NFRAG)
+    rate = rate_base + rate_base * jnp.minimum(step, 1000).astype(F32) / 1000.0
+    for block in range(4):
+        @pl.loop(0, 2)
+        def _(r):
+            rows = pl.ds(pl.multiple_of(block * 32 + r * 16, 16), 16)
+            first = beta_one * one_ref[0, rows, :] + (1.0 - beta_one) * grad_ref[rows, :]
+            grad = grad_ref[rows, :]
+            second = beta_two * two_ref[0, rows, :] + (1.0 - beta_two) * grad * grad
+            weight = weight_ref[0, rows, :].astype(F32)
+            update = first / (jnp.sqrt(second) + adam_eps) + decay_rate * weight
+            one_buf[rows, :] = first
+            two_buf[rows, :] = second
+            weight_buf[rows, :] = (weight - inner_rate * update).astype(BF16)
+
+        rows = pl.ds(block * 32, 32)
+        put(one_buf.at[rows, :], one_hbm.at[0, rows, :])
+        put(two_buf.at[rows, :], two_hbm.at[0, rows, :])
+        put(weight_buf.at[rows, :], weight_hbm.at[0, rows, :])
+
+    for block in range(2):
+        @pl.loop(0, 4)
+        def _(r):
+            rows = pl.ds(pl.multiple_of(block * 64 + r * 16, 16), 16)
+            anchor = anchors_ref[due, rows, :].astype(F32)
+            pseudo = anchor - drift_ref[rows, :].astype(F32) / N_ISLAND
+            momentum = outer_mu * momenta_ref[due, rows, :] + pseudo
+            momentum_buf[rows, :] = momentum
+            anchor_buf[rows, :] = (anchor - rate * (pseudo + outer_mu * momentum)).astype(BF16)
+
+        rows = pl.ds(block * 64, 64)
+        put(momentum_buf.at[rows, :], momentum_hbm.at[rows, :])
+        put(anchor_buf.at[rows, :], anchor_hbm.at[rows, :])
+    for copy in copies:
+        copy.wait()
+
+
+def finish(step, *operands):
+    inside = pl.BlockSpec(memory_space=pltpu.VMEM)
+    anywhere = pl.BlockSpec(memory_space=pl.ANY)
+    return pl.pallas_call(
+        finish_kernel,
+        out_shape=(
+            jax.ShapeDtypeStruct((TOK, D), BF16),
+            jax.ShapeDtypeStruct((1, ROWS, D), BF16),
+            jax.ShapeDtypeStruct((1, ROWS, D), F32),
+            jax.ShapeDtypeStruct((1, ROWS, D), F32),
+            jax.ShapeDtypeStruct((ROWS, D), BF16),
+            jax.ShapeDtypeStruct((ROWS, D), F32),
+        ),
+        in_specs=[pl.BlockSpec(memory_space=pltpu.SMEM)] + [inside] * 8,
+        out_specs=(anywhere,) * 6,
+        scratch_shapes=[
+            pltpu.VMEM((ROWS, D), BF16),
+            pltpu.VMEM((ROWS, D), F32),
+            pltpu.VMEM((ROWS, D), F32),
+            pltpu.VMEM((ROWS, D), BF16),
+            pltpu.VMEM((ROWS, D), F32),
+            pltpu.SemaphoreType.DMA((17,)),
+        ],
+        compiler_params=pltpu.CompilerParams(vmem_limit_bytes=16 * 2**20),
+        cost_estimate=pl.CostEstimate(
+            flops=30 * ROWS * D, bytes_accessed=12 * 2**20, transcendentals=ROWS * D
+        ),
+        name="finish",
+    )(step, *operands)
 
 
 def local(
@@ -608,20 +741,17 @@
     ctx_grad, weight_grad, drift = exchange(
         context, cotangent, norm_gain.reshape(1, D), out_weight, local_frags, outer_step
     )
-    first_new = beta_one * moment_one[0] + (1.0 - beta_one) * weight_grad
-    second_new = beta_two * moment_two[0] + (1.0 - beta_two) * weight_grad * weight_grad
-    weight_f = out_weight[0].astype(F32)
-    update = first_new / (jnp.sqrt(second_new) + adam_eps) + decay_rate * weight_f
-    new_weight = (weight_f - inner_rate * update).astype(BF16)
-    due_index = outer_step[0] % NFRAG
-    step_rate = rate_base + rate_base * jnp.minimum(outer_step[0], 1000).astype(F32) / 1000.0
-    anchor_due = lax.dynamic_index_in_dim(anchors, due_index, 0, keepdims=False).astype(F32)
-    moment_due = lax.dynamic_index_in_dim(outer_moment, due_index, 0, keepdims=False)
-    islands = lax.axis_size("island")
-    pseudo = anchor_due - drift.astype(F32) / islands
-    moment_new = outer_mu * moment_due + pseudo
-    anchor_new = (anchor_due - step_rate * (pseudo + outer_mu * moment_new)).astype(BF16)
-    return (ctx_grad, new_weight[None], first_new[None], second_new[None], anchor_new, moment_new)
+    return finish(
+        outer_step,
+        ctx_grad,
+        weight_grad,
+        drift,
+        moment_one,
+        moment_two,
+        out_weight,
+        anchors,
+        outer_moment,
+    )
 
 
 def solution(mesh):

time: 121 us -> 110 us (0.909)
  local copies, waits for them, and re-layouts: 6.39 us -> 0.02 us
  other arithmetic: 4.97 us -> 0 us
    unnamed x17 -> x10, local copies, waits for them, and re-layouts: 6.39 us -> 0.02 us
    convert_element_type x1 -> x0, other arithmetic: 2.72 us -> none  [local(): (anchor_due - step_rate * (pseudo + outer_mu * moment_new)).astype(BF16)]
    pallas_call x0 -> x1, Pallas kernels: none -> 2.47 us  [finish(): pl.pallas_call(finish_kernel, out_shape=(jax.ShapeDtypeStruct((TOK, D), B...]
    broadcast_in_dim x1 -> x0, other arithmetic: 2.25 us -> none  [local(): second_new[None]]
where the time goes in v2:
time: 110 us
  Pallas kernels  108 us (98%)
  between operations  1.37 us (1%)
    pallas_call x1, Pallas kernels, exchange(): pl.pallas_call(kernel, out_shape=(jax.ShapeDtypeStruct((TOK, D), BF16), j...  106 us
    pallas_call x1, Pallas kernels, finish(): pl.pallas_call(finish_kernel, out_shape=(jax.ShapeDtypeStruct((TOK, D), B...  2.47 us

profile of v2, /device:TPU:16, one launch (start us, length us, event | category | flops | bytes accessed | tf_op | source)
XLA Modules:
  0.0 109.8 jit_solution(4378675938380577254)
XLA Ops:
  1.3 0.0 copy-start
  1.3 0.0 copy-start.1
  1.3 0.0 copy-start.2
  1.3 0.0 copy-start.3
  1.3 0.0 copy-start.4
  1.3 105.9 %exchange.1 = (bf16[256,2048]{1,0:T(8,128)(2,1)S(1)}, f32[128,2048]{1,0:T(8,128)S(1)}, bf16[128,2048]{1,0:T(8,128)(2,1)S(1)}) custom-call(bf16[256,2048]{1,0:T(8,128)(2,1)} %ctx_hbm.1, bf16[256,2048]{1,0:T(8,128)(2,1)} %cot_hbm.1, f32[1,2048]{1,0:T(1,128)} %bitcast.1, bf16[1,128,2048]{2,1,0:T(8,128)(2,1)} %weight_ref.1, bf16[1,2,128,2048]{3,2,1,0:T(8,128)(2,1)} %frag_hbm.1, ...), custom_call_target="tpu_custom_call" | custom-call | flops 6442450944 | bytes 8388608 | tf_op jit(solution)/shard_map/exchange/pallas_call | solution.py:553
  107.3 0.0 copy-done
  107.3 0.0 copy-done.1
  107.3 0.0 copy-done.2
  107.3 0.0 copy-done.3
  107.3 0.0 copy-done.4
  107.3 2.5 %finish.1 = (bf16[256,2048]{1,0:T(8,128)(2,1)}, bf16[1,128,2048]{2,1,0:T(8,128)(2,1)}, f32[1,128,2048]{2,1,0:T(8,128)}, f32[1,128,2048]{2,1,0:T(8,128)}, bf16[128,2048]{1,0:T(8,128)(2,1)}, /*index=5*/f32[128,2048]{1,0:T(8,128)}) custom-call(s32[1]{0:T(128)S(6)} %copy.16.step_ref, bf16[256,2048]{1,0:T(8,128)(2,1)S(1)} %get-tuple-element.9.cg_ref, ...), custom_call_target="tpu_custom_call" | custom-call | flops 7864320 | bytes 12582912 | tf_op jit(solution)/shard_map/finish/pallas_call | solution.py:701
Async XLA Ops:
  1.3 106.0 %copy-start = (f32[2,128,2048]{2,1,0:T(8,128)S(1)}, f32[2,128,2048]{2,1,0:T(8,128)}, u32[]{:S(2)}) copy-start(f32[2,128,2048]{2,1,0:T(8,128)} %momenta_ref.1) | copy-start | bytes 6291460
  1.3 106.0 %copy-start.1 = (f32[1,128,2048]{2,1,0:T(8,128)S(1)}, f32[1,128,2048]{2,1,0:T(8,128)}, u32[]{:S(2)}) copy-start(f32[1,128,2048]{2,1,0:T(8,128)} %one_ref.1) | copy-start | bytes 3145732
  1.3 106.0 %copy-start.2 = (f32[1,128,2048]{2,1,0:T(8,128)S(1)}, f32[1,128,2048]{2,1,0:T(8,128)}, u32[]{:S(2)}) copy-start(f32[1,128,2048]{2,1,0:T(8,128)} %two_ref.1) | copy-start | bytes 3145732
  1.3 106.0 %copy-start.3 = (bf16[2,128,2048]{2,1,0:T(8,128)(2,1)S(1)}, bf16[2,128,2048]{2,1,0:T(8,128)(2,1)}, u32[]{:S(2)}) copy-start(bf16[2,128,2048]{2,1,0:T(8,128)(2,1)} %anchors_ref.1) | copy-start | bytes 3145732
  1.3 106.0 %copy-start.4 = (bf16[1,128,2048]{2,1,0:T(8,128)(2,1)S(1)}, bf16[1,128,2048]{2,1,0:T(8,128)(2,1)}, u32[]{:S(2)}) copy-start(bf16[1,128,2048]{2,1,0:T(8,128)(2,1)} %weight_ref.1) | copy-start | bytes 1572868

commit v3 on v2

--- a/solution.py
+++ b/solution.py
@@ -73,7 +73,6 @@
     sel,
     sum_a,
     sum_b,
-    sum_c,
     pass_a,
     pass_b,
     pass_c,
@@ -234,44 +233,29 @@
 
     def outer_3():
         arrive(got_c, as_sem.at[2], ar_sem.at[2])
-        total = sum_b[rows_of(xb * 16, 16), :] + got_c[...].astype(F32)
-        sum_c[...] = total
-        pass_c[...] = total.astype(BF16)
-        send(
-            pass_c.at[:, pl.ds(aligned(1 - yh, HALF), HALF)],
-            got_d,
-            as_sem.at[3],
-            ar_sem.at[3],
-            far_y,
-        )
+        pass_c[...] = (sum_b[rows_of(xb * 16, 16), :] + got_c[...].astype(F32)).astype(BF16)
+        send(pass_c, got_d, as_sem.at[3], ar_sem.at[3], far_y)
 
     def outer_4():
         arrive(got_d, as_sem.at[3], ar_sem.at[3])
-        cols = pl.ds(aligned(yh, HALF), HALF)
         rows = rows_of(row_c, 16)
-        drift[rows, cols] = (sum_c[:, cols] + got_d[...].astype(F32)).astype(BF16)
-        ref = drift.at[rows, cols]
-        send(ref, ref, as_sem.at[4], ar_sem.at[4], far_y)
+        drift[rows, :] = (pass_c[...].astype(F32) + got_d[...].astype(F32)).astype(BF16)
+        send(drift.at[rows, :], drift.at[rows, :], as_sem.at[4], ar_sem.at[4], far_x)
 
     def outer_5():
-        rows = rows_of(row_c, 16)
-        arrive(drift.at[rows, pl.ds(aligned(1 - yh, HALF), HALF)], as_sem.at[4], ar_sem.at[4])
-        send(drift.at[rows, :], drift.at[rows, :], as_sem.at[5], ar_sem.at[5], far_x)
+        arrive(drift.at[rows_of(row_b + (1 - xb) * 16, 16), :], as_sem.at[4], ar_sem.at[4])
+        rows = rows_of(row_b, 32)
+        send(drift.at[rows, :], drift.at[rows, :], as_sem.at[5], ar_sem.at[5], near_x)
 
     def outer_6():
-        arrive(drift.at[rows_of(row_b + (1 - xb) * 16, 16), :], as_sem.at[5], ar_sem.at[5])
-        rows = rows_of(row_b, 32)
-        send(drift.at[rows, :], drift.at[rows, :], as_sem.at[6], ar_sem.at[6], near_x)
+        arrive(drift.at[rows_of(row_a + (1 - xa) * 32, 32), :], as_sem.at[5], ar_sem.at[5])
+        rows = rows_of(row_a, 64)
+        send(drift.at[rows, :], drift.at[rows, :], as_sem.at[6], ar_sem.at[6], sib)
+
+    out_drift = pltpu.make_async_copy(drift, drift_hbm, out_sem.at[0])
 
     def outer_7():
-        arrive(drift.at[rows_of(row_a + (1 - xa) * 32, 32), :], as_sem.at[6], ar_sem.at[6])
-        rows = rows_of(row_a, 64)
-        send(drift.at[rows, :], drift.at[rows, :], as_sem.at[7], ar_sem.at[7], sib)
-
-    out_drift = pltpu.make_async_copy(drift, drift_hbm, out_sem.at[0])
-
-    def outer_8():
-        arrive(drift.at[rows_of((1 - core) * 64, 64), :], as_sem.at[7], ar_sem.at[7])
+        arrive(drift.at[rows_of((1 - core) * 64, 64), :], as_sem.at[6], ar_sem.at[6])
         out_drift.start()
 
     stat_recv[:, 8:128, :] = jnp.zeros((2, 120, TOK), F32)
@@ -307,7 +291,7 @@
     project(z, own_tok, first=True)
     turn(own_tok)
 
-    stages = (outer_1, outer_2, outer_3)
+    stages = (outer_1, outer_2)
     for hop in range(1, 4):
         froms = (chunk_at(-hop), chunk_at(hop))
         for u in range(4):
@@ -327,7 +311,8 @@
             project(froms[way], own_tok)
             if hop == 3:
                 project(froms[way], par_tok)
-        stages[hop - 1]()
+        if hop < 3:
+            stages[hop - 1]()
 
     def project_part(owner, tokens):
         rows = pl.ds(pl.multiple_of(chunk_at(4) * CHUNK + owner * ROWS, ROWS), ROWS)
@@ -376,6 +361,7 @@
             pair,
         )
 
+    outer_3()
     turn(par_tok)
     for half in range(2):
         k = stat_sem(1 - half)
@@ -498,23 +484,22 @@
 
     def after_3a():
         next_parts(2)
-        outer_4()
 
     def after_3b():
         own_back()
-        outer_5()
+        outer_4()
 
     def after_2a():
         next_parts(1)
-        outer_6()
+        outer_5()
 
     def after_2b():
         grad_of(chunk_rows(0), far)
-        outer_7()
+        outer_6()
 
     hop_of(3, (after_3a, after_3b))
     hop_of(2, (after_2a, after_2b))
-    hop_of(1, (outer_8, finish_back))
+    hop_of(1, (outer_7, finish_back))
 
     out_own = pltpu.make_async_copy(
         grad_out.at[0], grad_hbm.at[:, pl.ds(mine, HALF)], out_sem.at[2]
@@ -594,14 +579,13 @@
             pltpu.VMEM((ROWS, D), BF16),
             pltpu.VMEM((64, D), F32),
             pltpu.VMEM((32, D), F32),
-            pltpu.VMEM((16, D), F32),
             pltpu.VMEM((64, D), BF16),
             pltpu.VMEM((32, D), BF16),
             pltpu.VMEM((16, D), BF16),
             pltpu.VMEM((64, D), BF16),
             pltpu.VMEM((32, D), BF16),
             pltpu.VMEM((16, D), BF16),
-            pltpu.VMEM((16, HALF), BF16),
+            pltpu.VMEM((16, D), BF16),
             pltpu.VMEM((ROWS, D), BF16),
             dma((5,)),
             dma((4,)),
@@ -613,8 +597,8 @@
             dma((2, 2)),
             dma((2, 3, 4)),
             dma((2, 3, 4)),
-            dma((8,)),
-            dma((8,)),
+            dma((7,)),
+            dma((7,)),
         ],
         compiler_params=pltpu.CompilerParams(
             collective_id=0, has_side_effects=True, vmem_limit_bytes=46 * 2**20

time: 110 us -> 104 us (0.945)
  Pallas kernels: 108 us -> 102 us
    pallas_call x1, Pallas kernels: 106 us -> 99.6 us  [exchange(): pl.pallas_call(kernel, out_shape=(jax.ShapeDtypeStruct((TOK, D), BF16), j...]
where the time goes in v3:
time: 104 us
  Pallas kernels  102 us (98%)
  between operations  1.37 us (1%)
    pallas_call x1, Pallas kernels, exchange(): pl.pallas_call(kernel, out_shape=(jax.ShapeDtypeStruct((TOK, D), BF16), j...  99.6 us
    pallas_call x1, Pallas kernels, finish(): pl.pallas_call(finish_kernel, out_shape=(jax.ShapeDtypeStruct((TOK, D), B...  2.47 us

profile of v3, /device:TPU:16, one launch (start us, length us, event | category | flops | bytes accessed | tf_op | source)
XLA Modules:
  0.0 103.5 jit_solution(3168612407652440513)
XLA Ops:
  1.3 0.0 copy-start
  1.3 0.0 copy-start.1
  1.3 0.0 copy-start.2
  1.3 0.0 copy-start.3
  1.3 0.0 copy-start.4
  1.3 99.6 %exchange.1 = (bf16[256,2048]{1,0:T(8,128)(2,1)S(1)}, f32[128,2048]{1,0:T(8,128)S(1)}, bf16[128,2048]{1,0:T(8,128)(2,1)S(1)}) custom-call(bf16[256,2048]{1,0:T(8,128)(2,1)} %ctx_hbm.1, bf16[256,2048]{1,0:T(8,128)(2,1)} %cot_hbm.1, f32[1,2048]{1,0:T(1,128)} %bitcast.1, bf16[1,128,2048]{2,1,0:T(8,128)(2,1)} %weight_ref.1, bf16[1,2,128,2048]{3,2,1,0:T(8,128)(2,1)} %frag_hbm.1, ...), custom_call_target="tpu_custom_call" | custom-call | flops 6442450944 | bytes 8388608 | tf_op jit(solution)/shard_map/exchange/pallas_call | solution.py:538
  101.0 0.0 copy-done
  101.0 0.0 copy-done.1
  101.0 0.0 copy-done.2
  101.0 0.0 copy-done.3
  101.0 0.0 copy-done.4
  101.0 2.5 %finish.1 = (bf16[256,2048]{1,0:T(8,128)(2,1)}, bf16[1,128,2048]{2,1,0:T(8,128)(2,1)}, f32[1,128,2048]{2,1,0:T(8,128)}, f32[1,128,2048]{2,1,0:T(8,128)}, bf16[128,2048]{1,0:T(8,128)(2,1)}, /*index=5*/f32[128,2048]{1,0:T(8,128)}) custom-call(s32[1]{0:T(128)S(6)} %copy.16.step_ref, bf16[256,2048]{1,0:T(8,128)(2,1)S(1)} %get-tuple-element.9.cg_ref, ...), custom_call_target="tpu_custom_call" | custom-call | flops 7864320 | bytes 12582912 | tf_op jit(solution)/shard_map/finish/pallas_call | solution.py:685
Async XLA Ops:
  1.3 99.7 %copy-start = (f32[2,128,2048]{2,1,0:T(8,128)S(1)}, f32[2,128,2048]{2,1,0:T(8,128)}, u32[]{:S(2)}) copy-start(f32[2,128,2048]{2,1,0:T(8,128)} %momenta_ref.1) | copy-start | bytes 6291460
  1.3 99.7 %copy-start.1 = (f32[1,128,2048]{2,1,0:T(8,128)S(1)}, f32[1,128,2048]{2,1,0:T(8,128)}, u32[]{:S(2)}) copy-start(f32[1,128,2048]{2,1,0:T(8,128)} %one_ref.1) | copy-start | bytes 3145732
  1.3 99.7 %copy-start.2 = (f32[1,128,2048]{2,1,0:T(8,128)S(1)}, f32[1,128,2048]{2,1,0:T(8,128)}, u32[]{:S(2)}) copy-start(f32[1,128,2048]{2,1,0:T(8,128)} %two_ref.1) | copy-start | bytes 3145732
  1.3 99.7 %copy-start.3 = (bf16[2,128,2048]{2,1,0:T(8,128)(2,1)S(1)}, bf16[2,128,2048]{2,1,0:T(8,128)(2,1)}, u32[]{:S(2)}) copy-start(bf16[2,128,2048]{2,1,0:T(8,128)(2,1)} %anchors_ref.1) | copy-start | bytes 3145732
  1.3 99.7 %copy-start.4 = (bf16[1,128,2048]{2,1,0:T(8,128)(2,1)S(1)}, bf16[1,128,2048]{2,1,0:T(8,128)(2,1)}, u32[]{:S(2)}) copy-start(bf16[1,128,2048]{2,1,0:T(8,128)(2,1)} %weight_ref.1) | copy-start | bytes 1572868

commit v4 on v3

--- a/solution.py
+++ b/solution.py
@@ -110,7 +110,8 @@
     pair = (isl, z * 2 + other)
     sib = (isl + 1 - 2 * core, fsd)
     near_x = (isl + 2 - 4 * xa, fsd)
-    far_x = (isl + 4 - 8 * xb, fsd)
+    far_x = (isl + 6 - 4 * x, fsd)
+    part = lax.rem(xa + xb, 2)
     far_y = (isl + 8 - 16 * yh, fsd)
     mine = aligned(y, HALF)
     theirs = aligned(other, HALF)
@@ -188,7 +189,7 @@
     )
 
     row_a = core * 64
-    row_b = row_a + xa * 32
+    row_b = row_a + part * 32
     row_c = row_b + xb * 16
 
     def rows_of(start, size):
@@ -217,7 +218,7 @@
             sum_a[rows, :] = total
             pass_a[rows, :] = total.astype(BF16)
 
-        send(pass_a.at[rows_of((1 - xa) * 32, 32), :], got_b, as_sem.at[1], ar_sem.at[1], near_x)
+        send(pass_a.at[rows_of((1 - part) * 32, 32), :], got_b, as_sem.at[1], ar_sem.at[1], near_x)
 
     def outer_2():
         arrive(got_b, as_sem.at[1], ar_sem.at[1])
@@ -225,7 +226,7 @@
         @pl.loop(0, 2)
         def _(r):
             rows = rows_of(r * 16, 16)
-            total = sum_a[rows_of(xa * 32 + r * 16, 16), :] + got_b[rows, :].astype(F32)
+            total = sum_a[rows_of(part * 32 + r * 16, 16), :] + got_b[rows, :].astype(F32)
             sum_b[rows, :] = total
             pass_b[rows, :] = total.astype(BF16)
 
@@ -248,7 +249,7 @@
         send(drift.at[rows, :], drift.at[rows, :], as_sem.at[5], ar_sem.at[5], near_x)
 
     def outer_6():
-        arrive(drift.at[rows_of(row_a + (1 - xa) * 32, 32), :], as_sem.at[5], ar_sem.at[5])
+        arrive(drift.at[rows_of(row_a + (1 - part) * 32, 32), :], as_sem.at[5], ar_sem.at[5])
         rows = rows_of(row_a, 64)
         send(drift.at[rows, :], drift.at[rows, :], as_sem.at[6], ar_sem.at[6], sib)
 
@@ -259,6 +260,7 @@
         out_drift.start()
 
     stat_recv[:, 8:128, :] = jnp.zeros((2, 120, TOK), F32)
+    stat_send[...] = jnp.zeros((2, 8, TOK), F32)
     outer_0()
 
     def chunk_at(offset):
@@ -270,7 +272,7 @@
     def project(chunk, tokens, first=False):
         rows = pl.ds(aligned(chunk, CHUNK), CHUNK)
 
-        @pl.loop(0, 4)
+        @pl.loop(0, 4, unroll=True)
         def _(n):
             cols = pl.ds(aligned(n, 256), 256)
             part = jnp.dot(ctx[tokens, rows], wbuf[rows, cols], preferred_element_type=F32)
@@ -317,7 +319,7 @@
     def project_part(owner, tokens):
         rows = pl.ds(pl.multiple_of(chunk_at(4) * CHUNK + owner * ROWS, ROWS), ROWS)
 
-        @pl.loop(0, 4)
+        @pl.loop(0, 4, unroll=True)
         def _(n):
             cols = pl.ds(aligned(n, 256), 256)
             proj[tokens, cols] += jnp.dot(
@@ -334,7 +336,6 @@
             arrive(cot.at[par_tok, :], ys_sem.at[3], yr_sem.at[3])
 
     gain = gain_buf[...]
-    lane = lax.broadcasted_iota(jnp.int32, (UNIT, 128), 1)
 
     def stat_sem(half):
         return 4 if half == 1 else 11
@@ -342,16 +343,19 @@
     for half in (1, 0):
         project_part(other, pl.ds(half * TOK, TOK))
 
-        @pl.loop(0, TOK // UNIT)
+        @pl.loop(0, TOK // UNIT, unroll=True)
         def _(r):
             rows = rows_of(half * TOK + r * UNIT, UNIT)
             p = proj[rows, :]
             scaled = cot[rows, :].astype(F32) * gain
-            square = jnp.sum(p * p, axis=1, keepdims=True)
-            cross = jnp.sum(scaled * p, axis=1, keepdims=True)
-            stat_own[rows, :] = jnp.where(lane == 0, square, jnp.where(lane == 1, cross, 0.0))
-
-        stat_send[half] = stat_own[half * TOK : half * TOK + TOK, :].T[0:8, :]
+            square, cross = p * p, scaled * p
+            lanes = [slice(128 * i, 128 * i + 128) for i in range(HALF // 128)]
+            stat_own[0, rows, :] = sum(square[:, i] for i in lanes)
+            stat_own[1, rows, :] = sum(cross[:, i] for i in lanes)
+
+        for n in range(2):
+            turned = stat_own[n, half * TOK : half * TOK + TOK, :].T
+            stat_send[half, n : n + 1, :] = jnp.sum(turned, axis=0, keepdims=True)
         k = stat_sem(half)
         send(
             stat_send.at[half],
@@ -366,19 +370,20 @@
     for half in range(2):
         k = stat_sem(1 - half)
         arrive(stat_recv.at[half, pl.ds(0, 8), :], ys_sem.at[k], yr_sem.at[k])
-        stat_own[half * TOK : half * TOK + TOK, :] += stat_recv[half].T
-
-        @pl.loop(0, TOK // UNIT)
+        stat_recv[half, 0:2, :] += stat_send[half, 0:2, :]
+        stat_own[0, half * TOK : half * TOK + TOK, :] = stat_recv[half].T
+
+        @pl.loop(0, TOK // UNIT, unroll=True)
         def _(r):
             rows = rows_of(half * TOK + r * UNIT, UNIT)
-            stat = stat_own[rows, :] * (1.0 / D)
+            stat = stat_own[0, rows, :] * (1.0 / D)
             inv = lax.rsqrt(stat[:, 0:1] + 1e-06)
             slope = inv * inv * stat[:, 1:2]
             scaled = cot[rows, :].astype(F32) * gain
             pg[rows, :] = (inv * (scaled - proj[rows, :] * slope)).astype(BF16)
 
     def grad_of(rows, dst):
-        @pl.loop(0, 4)
+        @pl.loop(0, 4, unroll=True)
         def _(n):
             cols = pl.ds(aligned(n, 256), 256)
             dst[:, cols] = jnp.dot(ctxt[rows, :], pg[:, cols], preferred_element_type=F32)
@@ -559,7 +564,7 @@
             pltpu.VMEM((PAIR, HALF), F32),
             pltpu.VMEM((PAIR, HALF), BF16),
             pltpu.VMEM((D, PAIR), BF16),
-            pltpu.VMEM((PAIR, 128), F32),
+            pltpu.VMEM((2, PAIR, 128), F32),
             pltpu.VMEM((2, 8, TOK), F32),
             pltpu.VMEM((2, 128, TOK), F32),
             pltpu.VMEM((CHUNK, HALF), F32),
@@ -644,8 +649,21 @@
     step = step_ref[0]
     due = lax.rem(step, NFRAG)
     rate = rate_base + rate_base * jnp.minimum(step, 1000).astype(F32) / 1000.0
+    for block in range(2):
+        @pl.loop(0, 4)
+        def _(r):
+            rows = pl.ds(pl.multiple_of(block * 64 + r * 16, 16), 16)
+            anchor = anchors_ref[due, rows, :].astype(F32)
+            pseudo = anchor - drift_ref[rows, :].astype(F32) / N_ISLAND
+            momentum = outer_mu * momenta_ref[due, rows, :] + pseudo
+            momentum_buf[rows, :] = momentum
+            anchor_buf[rows, :] = (anchor - rate * (pseudo + outer_mu * momentum)).astype(BF16)
+
+        rows = pl.ds(block * 64, 64)
+        put(momentum_buf.at[rows, :], momentum_hbm.at[rows, :])
+        put(anchor_buf.at[rows, :], anchor_hbm.at[rows, :])
     for block in range(4):
-        @pl.loop(0, 2)
+        @pl.loop(0, 2, unroll=True)
         def _(r):
             rows = pl.ds(pl.multiple_of(block * 32 + r * 16, 16), 16)
             first = beta_one * one_ref[0, rows, :] + (1.0 - beta_one) * grad_ref[rows, :]
@@ -662,19 +680,6 @@
         put(two_buf.at[rows, :], two_hbm.at[0, rows, :])
         put(weight_buf.at[rows, :], weight_hbm.at[0, rows, :])
 
-    for block in range(2):
-        @pl.loop(0, 4)
-        def _(r):
-            rows = pl.ds(pl.multiple_of(block * 64 + r * 16, 16), 16)
-            anchor = anchors_ref[due, rows, :].astype(F32)
-            pseudo = anchor - drift_ref[rows, :].astype(F32) / N_ISLAND
-            momentum = outer_mu * momenta_ref[due, rows, :] + pseudo
-            momentum_buf[rows, :] = momentum
-            anchor_buf[rows, :] = (anchor - rate * (pseudo + outer_mu * momentum)).astype(BF16)
-
-        rows = pl.ds(block * 64, 64)
-        put(momentum_buf.at[rows, :], momentum_hbm.at[rows, :])
-        put(anchor_buf.at[rows, :], anchor_hbm.at[rows, :])
     for copy in copies:
         copy.wait()
 

time: 104 us -> 99.7 us (0.959)
  Pallas kernels: 102 us -> 97.8 us
    pallas_call x1, Pallas kernels: 99.6 us -> 95.3 us  [exchange(): pl.pallas_call(kernel, out_shape=(jax.ShapeDtypeStruct((TOK, D), BF16), j...]
where the time goes in v4:
time: 99.7 us; the launch traced here: 99.2 us
  Pallas kernels  97.8 us (98%)
  between operations  1.37 us (1%)
    pallas_call x1, Pallas kernels, exchange(): pl.pallas_call(kernel, out_shape=(jax.ShapeDtypeStruct((TOK, D), BF16), j...  95.3 us
    pallas_call x1, Pallas kernels, finish(): pl.pallas_call(finish_kernel, out_shape=(jax.ShapeDtypeStruct((TOK, D), B...  2.46 us

profile of v4, /device:TPU:16, one launch (start us, length us, event | category | flops | bytes accessed | tf_op | source)
XLA Modules:
  0.0 99.2 jit_solution(13311951349596447825)
XLA Ops:
  1.3 0.0 copy-start
  1.3 0.0 copy-start.1
  1.3 0.0 copy-start.2
  1.3 0.0 copy-start.3
  1.3 0.0 copy-start.4
  1.3 95.3 %exchange.1 = (bf16[256,2048]{1,0:T(8,128)(2,1)S(1)}, f32[128,2048]{1,0:T(8,128)S(1)}, bf16[128,2048]{1,0:T(8,128)(2,1)S(1)}) custom-call(bf16[256,2048]{1,0:T(8,128)(2,1)} %ctx_hbm.1, bf16[256,2048]{1,0:T(8,128)(2,1)} %cot_hbm.1, f32[1,2048]{1,0:T(1,128)} %bitcast.1, bf16[1,128,2048]{2,1,0:T(8,128)(2,1)} %weight_ref.1, bf16[1,2,128,2048]{3,2,1,0:T(8,128)(2,1)} %frag_hbm.1, ...), custom_call_target="tpu_custom_call" | custom-call | flops 6442450944 | bytes 8388608 | tf_op jit(solution)/shard_map/exchange/pallas_call | solution.py:543
  96.7 0.0 copy-done
  96.7 0.0 copy-done.1
  96.7 0.0 copy-done.2
  96.7 0.0 copy-done.3
  96.7 0.0 copy-done.4
  96.7 2.5 %finish.1 = (bf16[256,2048]{1,0:T(8,128)(2,1)}, bf16[1,128,2048]{2,1,0:T(8,128)(2,1)}, f32[1,128,2048]{2,1,0:T(8,128)}, f32[1,128,2048]{2,1,0:T(8,128)}, bf16[128,2048]{1,0:T(8,128)(2,1)}, /*index=5*/f32[128,2048]{1,0:T(8,128)}) custom-call(s32[1]{0:T(128)S(6)} %copy.16.step_ref, bf16[256,2048]{1,0:T(8,128)(2,1)S(1)} %get-tuple-element.9.cg_ref, ...), custom_call_target="tpu_custom_call" | custom-call | flops 7864320 | bytes 12582912 | tf_op jit(solution)/shard_map/finish/pallas_call | solution.py:690
Async XLA Ops:
  1.3 95.4 %copy-start = (f32[2,128,2048]{2,1,0:T(8,128)S(1)}, f32[2,128,2048]{2,1,0:T(8,128)}, u32[]{:S(2)}) copy-start(f32[2,128,2048]{2,1,0:T(8,128)} %momenta_ref.1) | copy-start | bytes 6291460
  1.3 95.4 %copy-start.1 = (f32[1,128,2048]{2,1,0:T(8,128)S(1)}, f32[1,128,2048]{2,1,0:T(8,128)}, u32[]{:S(2)}) copy-start(f32[1,128,2048]{2,1,0:T(8,128)} %one_ref.1) | copy-start | bytes 3145732
  1.3 95.4 %copy-start.2 = (f32[1,128,2048]{2,1,0:T(8,128)S(1)}, f32[1,128,2048]{2,1,0:T(8,128)}, u32[]{:S(2)}) copy-start(f32[1,128,2048]{2,1,0:T(8,128)} %two_ref.1) | copy-start | bytes 3145732
  1.3 95.4 %copy-start.3 = (bf16[2,128,2048]{2,1,0:T(8,128)(2,1)S(1)}, bf16[2,128,2048]{2,1,0:T(8,128)(2,1)}, u32[]{:S(2)}) copy-start(bf16[2,128,2048]{2,1,0:T(8,128)(2,1)} %anchors_ref.1) | copy-start | bytes 3145732
  1.3 95.4 %copy-start.4 = (bf16[1,128,2048]{2,1,0:T(8,128)(2,1)S(1)}, bf16[1,128,2048]{2,1,0:T(8,128)(2,1)}, u32[]{:S(2)}) copy-start(bf16[1,128,2048]{2,1,0:T(8,128)(2,1)} %weight_ref.1) | copy-start | bytes 1572868

commit v5 on v4

--- a/solution.py
+++ b/solution.py
@@ -43,8 +43,8 @@
     w_hbm,
     frag_hbm,
     step_ref,
-    cg_hbm,
-    grad_hbm,
+    cg_ref,
+    grad_ref,
     drift_hbm,
     wbuf,
     ctx,
@@ -64,11 +64,9 @@
     full_recv,
     y_send,
     y_recv,
-    grad_out,
     cg_own,
     cg_send,
     cg_recv,
-    cg_out,
     frag,
     sel,
     sum_a,
@@ -130,6 +128,10 @@
             src_ref=dst, dst_ref=dst, send_sem=ss, recv_sem=rs, device_id=pair, device_id_type=MESH
         ).wait_recv()
 
+    barrier = pltpu.get_barrier_semaphore()
+    for dev in (far_x, up, down, far_y, pair, near_x, sib):
+        pl.semaphore_signal(barrier, inc=1, device_id=dev, device_id_type=MESH)
+
     loc_w = pltpu.make_async_copy(
         w_hbm.at[0, :, pl.ds(mine, HALF)], wbuf.at[pl.ds(aligned(fsd, ROWS), ROWS), :], loc_sem.at[0]
     )
@@ -142,9 +144,6 @@
     for copy in (loc_w, loc_frag, loc_ctx, loc_cot, loc_gain):
         copy.start()
 
-    barrier = pltpu.get_barrier_semaphore()
-    for dev in (up, down, pair, sib, near_x, far_x, far_y):
-        pl.semaphore_signal(barrier, inc=1, device_id=dev, device_id_type=MESH)
     pl.semaphore_wait(barrier, 7)
 
     def unit_rows(z_from, u):
@@ -462,8 +461,6 @@
             cols = pl.ds(aligned(n, 256), 256)
             cg_own[:, cols] = back(own_tok, cols)
 
-    out_cg = pltpu.make_async_copy(cg_out, cg_hbm, out_sem.at[1])
-
     def finish_back():
         for q in range(4):
             cols = pl.ds(q * 512, 512)
@@ -472,68 +469,63 @@
         @pl.loop(0, 16)
         def _(r):
             rows = rows_of(r * 16, 16)
-            cg_out[rows, :] = (cg_own[rows, :] + cg_recv[rows, :].astype(F32)).astype(BF16)
-
-        out_cg.start()
-
-    def hop_of(hop, between):
-        for piece in range(2):
-            for t in range(2):
-                for way in range(2):
-                    forward(hop, piece, t, way)
-            between[piece]()
+            cg_ref[rows, :] = (cg_own[rows, :] + cg_recv[rows, :].astype(F32)).astype(BF16)
 
     def next_parts(hop):
         for way in range(2):
             grad_of(chunk_rows(hop if way == 0 else -hop), parts.at[way, 3 - hop])
 
-    def after_3a():
-        next_parts(2)
-
-    def after_3b():
-        own_back()
-        outer_4()
-
-    def after_2a():
-        next_parts(1)
-        outer_5()
-
-    def after_2b():
-        grad_of(chunk_rows(0), far)
-        outer_6()
-
-    hop_of(3, (after_3a, after_3b))
-    hop_of(2, (after_2a, after_2b))
-    hop_of(1, (outer_7, finish_back))
-
-    out_own = pltpu.make_async_copy(
-        grad_out.at[0], grad_hbm.at[:, pl.ds(mine, HALF)], out_sem.at[2]
-    )
-    out_par = pltpu.make_async_copy(
-        grad_out.at[1], grad_hbm.at[:, pl.ds(theirs, HALF)], out_sem.at[3]
-    )
-    for piece in range(2):
-        for t in range(2):
-            n = 2 * piece + t
-            rows = pl.ds(t * UNIT, UNIT)
-            total = far[piece_rows(piece, UNIT, t * UNIT), :]
-            for way in range(2):
-                arrive(full_recv.at[way, 2, n], fs_sem.at[way, 2, n], fr_sem.at[way, 2, n])
-                total = total + full_recv[way, 2, n].astype(F32)
-            if piece == 0:
-                y_send[t] = total.astype(BF16)
-                send(y_send.at[t], y_recv.at[t], ys_sem.at[9 + t], yr_sem.at[9 + t], pair)
-            else:
-                grad_out[0, rows, :] = total
-    out_own.start()
-    for t in range(2):
+    def both(hop, piece, t):
+        for way in range(2):
+            forward(hop, piece, t, way)
+
+    def settle(piece, t):
+        n = 2 * piece + t
+        rows = pl.ds(t * UNIT, UNIT)
+        total = far[piece_rows(piece, UNIT, t * UNIT), :]
+        for way in range(2):
+            arrive(full_recv.at[way, 2, n], fs_sem.at[way, 2, n], fr_sem.at[way, 2, n])
+            total = total + full_recv[way, 2, n].astype(F32)
+        if piece == 0:
+            y_send[t] = total.astype(BF16)
+            send(y_send.at[t], y_recv.at[t], ys_sem.at[9 + t], yr_sem.at[9 + t], pair)
+        else:
+            grad_ref[rows, pl.ds(mine, HALF)] = total
+
+    def take(t):
         arrive(y_recv.at[t], ys_sem.at[9 + t], yr_sem.at[9 + t])
-        grad_out[1, t * UNIT : (t + 1) * UNIT, :] = y_recv[t].astype(F32)
-    out_par.start()
+        grad_ref[t * UNIT : (t + 1) * UNIT, pl.ds(theirs, HALF)] = y_recv[t].astype(F32)
+
+    both(3, 0, 0)
+    both(3, 0, 1)
+    next_parts(2)
+    both(3, 1, 0)
+    both(3, 1, 1)
+    own_back()
+    outer_4()
+    both(2, 0, 0)
+    both(2, 0, 1)
+    next_parts(1)
+    both(2, 1, 0)
+    outer_5()
+    both(1, 0, 0)
+    both(1, 0, 1)
+    both(2, 1, 1)
+    grad_of(chunk_rows(0), far)
+    outer_6()
+    both(1, 1, 0)
+    settle(0, 0)
+    finish_back()
+    settle(0, 1)
+    both(1, 1, 1)
+    outer_7()
+    settle(1, 0)
+    take(0)
+    take(1)
+    settle(1, 1)
     for copy in sends:
         copy.wait_send()
-    for copy in (out_drift, out_cg, out_own, out_par):
-        copy.wait()
+    out_drift.wait()
 
 
 def exchange(context, cotangent, gain, weight, frags, step):
@@ -555,7 +547,11 @@
             in_hbm,
             pl.BlockSpec(memory_space=pltpu.SMEM),
         ],
-        out_specs=(anywhere, anywhere, anywhere),
+        out_specs=(
+            pl.BlockSpec(memory_space=pltpu.VMEM),
+            pl.BlockSpec(memory_space=pltpu.VMEM),
+            anywhere,
+        ),
         scratch_shapes=[
             pltpu.VMEM((D, HALF), BF16),
             pltpu.VMEM((PAIR, D), BF16),
@@ -575,9 +571,7 @@
             pltpu.VMEM((2, 3, 4, UNIT, HALF), BF16),
             pltpu.VMEM((2, UNIT, HALF), BF16),
             pltpu.VMEM((2, UNIT, HALF), BF16),
-            pltpu.VMEM((2, ROWS, HALF), F32),
             pltpu.VMEM((TOK, D), F32),
-            pltpu.VMEM((TOK, D), BF16),
             pltpu.VMEM((TOK, D), BF16),
             pltpu.VMEM((TOK, D), BF16),
             pltpu.VMEM((NFRAG, ROWS, D), BF16),
@@ -593,7 +587,7 @@
             pltpu.VMEM((16, D), BF16),
             pltpu.VMEM((ROWS, D), BF16),
             dma((5,)),
-            dma((4,)),
+            dma((1,)),
             dma((2, 4, 4)),
             dma((2, 4, 4)),
             dma((12,)),

time: 99.7 us -> 99.4 us (level)
  no operation moved by 1% of the time
where the time goes in v5:
time: 99.4 us; the launch traced here: 99.3 us
  Pallas kernels  97.9 us (98%)
  between operations  1.37 us (1%)
    pallas_call x1, Pallas kernels, exchange(): pl.pallas_call(kernel, out_shape=(jax.ShapeDtypeStruct((TOK, D), BF16), j...  95.5 us
    pallas_call x1, Pallas kernels, finish(): pl.pallas_call(finish_kernel, out_shape=(jax.ShapeDtypeStruct((TOK, D), B...  2.46 us

profile of v5, /device:TPU:16, one launch (start us, length us, event | category | flops | bytes accessed | tf_op | source)
XLA Modules:
  0.0 99.3 jit_solution(285520076049646649)
XLA Ops:
  1.3 0.0 copy-start
  1.3 0.0 copy-start.1
  1.3 0.0 copy-start.2
  1.3 0.0 copy-start.3
  1.3 0.0 copy-start.4
  1.3 95.5 %exchange.1 = (bf16[256,2048]{1,0:T(8,128)(2,1)S(1)}, f32[128,2048]{1,0:T(8,128)S(1)}, bf16[128,2048]{1,0:T(8,128)(2,1)S(1)}) custom-call(bf16[256,2048]{1,0:T(8,128)(2,1)} %ctx_hbm.1, bf16[256,2048]{1,0:T(8,128)(2,1)} %cot_hbm.1, f32[1,2048]{1,0:T(1,128)} %bitcast.1, bf16[1,128,2048]{2,1,0:T(8,128)(2,1)} %weight_ref.1, bf16[1,2,128,2048]{3,2,1,0:T(8,128)(2,1)} %frag_hbm.1, ...), custom_call_target="tpu_custom_call" | custom-call | flops 6442450944 | bytes 8388608 | tf_op jit(solution)/shard_map/exchange/pallas_call | solution.py:535
  96.8 0.0 copy-done
  96.8 0.0 copy-done.1
  96.8 0.0 copy-done.2
  96.8 0.0 copy-done.3
  96.8 0.0 copy-done.4
  96.9 2.5 %finish.1 = (bf16[256,2048]{1,0:T(8,128)(2,1)}, bf16[1,128,2048]{2,1,0:T(8,128)(2,1)}, f32[1,128,2048]{2,1,0:T(8,128)}, f32[1,128,2048]{2,1,0:T(8,128)}, bf16[128,2048]{1,0:T(8,128)(2,1)}, /*index=5*/f32[128,2048]{1,0:T(8,128)}) custom-call(s32[1]{0:T(128)S(6)} %copy.16.step_ref, bf16[256,2048]{1,0:T(8,128)(2,1)S(1)} %get-tuple-element.9.cg_ref, ...), custom_call_target="tpu_custom_call" | custom-call | flops 7864320 | bytes 12582912 | tf_op jit(solution)/shard_map/finish/pallas_call | solution.py:684
Async XLA Ops:
  1.3 95.5 %copy-start = (f32[2,128,2048]{2,1,0:T(8,128)S(1)}, f32[2,128,2048]{2,1,0:T(8,128)}, u32[]{:S(2)}) copy-start(f32[2,128,2048]{2,1,0:T(8,128)} %momenta_ref.1) | copy-start | bytes 6291460
  1.3 95.5 %copy-start.1 = (f32[1,128,2048]{2,1,0:T(8,128)S(1)}, f32[1,128,2048]{2,1,0:T(8,128)}, u32[]{:S(2)}) copy-start(f32[1,128,2048]{2,1,0:T(8,128)} %one_ref.1) | copy-start | bytes 3145732
  1.3 95.5 %copy-start.2 = (f32[1,128,2048]{2,1,0:T(8,128)S(1)}, f32[1,128,2048]{2,1,0:T(8,128)}, u32[]{:S(2)}) copy-start(f32[1,128,2048]{2,1,0:T(8,128)} %two_ref.1) | copy-start | bytes 3145732
  1.3 95.5 %copy-start.3 = (bf16[2,128,2048]{2,1,0:T(8,128)(2,1)S(1)}, bf16[2,128,2048]{2,1,0:T(8,128)(2,1)}, u32[]{:S(2)}) copy-start(bf16[2,128,2048]{2,1,0:T(8,128)(2,1)} %anchors_ref.1) | copy-start | bytes 3145732
  1.3 95.5 %copy-start.4 = (bf16[1,128,2048]{2,1,0:T(8,128)(2,1)S(1)}, bf16[1,128,2048]{2,1,0:T(8,128)(2,1)}, u32[]{:S(2)}) copy-start(bf16[1,128,2048]{2,1,0:T(8,128)(2,1)} %weight_ref.1) | copy-start | bytes 1572868
